TPU v7x, 512 devices: a whole 4x8x8 slice. The times are simulated.
512 devices in a mesh: exp: 8 (over x, y_hi), rows: 64 (over z, y_lo, core).
Axes of the slice: x: 4, y: 8 (y_hi: 2, y_lo: 4; y = y_hi * 4 + y_lo), z: 8, core: 2. Of those that a mesh axis runs over, the one named last changes fastest.
Arguments:
- calib: bfloat16 [20480, 5120], P('rows'), may hold values from -16 to 16
- target: bfloat16 [20480, 768], P('rows', 'exp'), may hold values from -6 to 6
- route: int32 [20480], P('rows'), may hold values from 0 to 7
- base: bfloat16 [5120, 768], P('rows', 'exp'), may hold values from -5 to 5
- up_factor: bfloat16 [8, 5120, 64], P('exp'), may hold values from -3 to 3
- down_factor: bfloat16 [8, 64, 768], P('exp'), may hold values from -3 to 3
Outputs:
- new_base: bfloat16 [5120, 768], P('rows', 'exp')
- new_up: bfloat16 [8, 5120, 64], P('exp')
- new_down: bfloat16 [8, 64, 768], P('exp')
All inputs are finite; a program needn't handle non-finite values.
Results may differ from a plain program's by a relative error of at most 0.02.
Values may be sent and summed in bfloat16 or wider, within the bound.
A program may use at most 64 MiB of HBM per device.

v0:
```python
import math

import jax
import jax.numpy as jnp
from jax import lax
from jax.sharding import PartitionSpec as P

ITERS = 2


step_rate = 0.25


def body(calib, target, route, base, up_factor, down_factor):
    tok_rows, width = calib.shape
    rank = up_factor.shape[2]
    groups = lax.axis_size("exp")
    inv_d = 1.0 / math.sqrt(width)
    inv_r = 1.0 / math.sqrt(rank)
    inv_t = 1.0 / math.sqrt(tok_rows * lax.axis_size("rows"))
    mine = (route == lax.axis_index("exp"))[:, None]
    target_wide = target.astype(jnp.float32)
    up_now = up_factor[0]
    down_now = down_factor[0]
    for step in range(ITERS):
        base_cols = jnp.dot(
            calib,
            lax.all_gather(base, "rows", axis=0, tiled=True),
            preferred_element_type=jnp.float32,
        )
        base_cols = (base_cols * inv_d).astype(jnp.bfloat16)
        inner = (jnp.dot(calib, up_now, preferred_element_type=jnp.float32) * inv_d).astype(
            jnp.bfloat16
        )
        inner = jnp.where(mine, inner, jnp.zeros_like(inner))
        delta = (jnp.dot(inner, down_now, preferred_element_type=jnp.float32) * inv_r).astype(
            jnp.bfloat16
        )
        moved = lax.all_to_all(delta, "exp", split_axis=1, concat_axis=0, tiled=True)
        delta_cols = jnp.sum(moved.reshape(groups, tok_rows, -1).astype(jnp.float32), axis=0)
        resid_cols = (base_cols.astype(jnp.float32) + delta_cols - target_wide).astype(jnp.bfloat16)
        resid_full = lax.all_gather(resid_cols, "exp", axis=1, tiled=True)
        resid_mine = jnp.where(mine, resid_full, jnp.zeros_like(resid_full))
        back = lax.dot_general(
            resid_mine, down_now, (((1,), (1,)), ((), ())), preferred_element_type=jnp.float32
        )
        back = (back * inv_r).astype(jnp.bfloat16)
        grad_base = lax.psum_scatter(
            lax.dot_general(
                calib, resid_cols, (((0,), (0,)), ((), ())), preferred_element_type=jnp.float32
            )
            * inv_t,
            "rows",
            scatter_dimension=0,
            tiled=True,
        )
        grad_up = (
            lax.dot_general(
                calib, back, (((0,), (0,)), ((), ())), preferred_element_type=jnp.float32
            )
            * inv_t
        )
        grad_down = (
            lax.dot_general(
                inner, resid_mine, (((0,), (0,)), ((), ())), preferred_element_type=jnp.float32
            )
            * inv_t
        )
        grad_up, grad_down = lax.psum((grad_up, grad_down), "rows")
        base = (base.astype(jnp.float32) - step_rate * grad_base).astype(jnp.bfloat16)
        up_now = (up_now.astype(jnp.float32) - step_rate * grad_up).astype(jnp.bfloat16)
        down_now = (down_now.astype(jnp.float32) - step_rate * grad_down).astype(jnp.bfloat16)
    return (base, up_now[None], down_now[None])


def solution(mesh):
    in_specs = (
        P("rows", None),
        P("rows", "exp"),
        P("rows"),
        P("rows", "exp"),
        P("exp", None, None),
        P("exp", None, None),
    )
    out_specs = (P("rows", "exp"), P("exp", None, None), P("exp", None, None))
    return jax.shard_map(body, mesh=mesh, in_specs=in_specs, out_specs=out_specs, check_vma=False)
```

profile of v0, /device:TPU:1, one launch (start us, length us, event | category | flops | bytes accessed | tf_op | source)
XLA Modules:
  0.0 1978.7 jit_solution(84160103791882234)
XLA Ops:
  7.2 0.0 copy-start
  7.2 0.8 broadcast_compare_fusion
  8.0 1.1 copy-done
  9.1 0.0 copy-start.2
  9.1 2.2 fusion.22
  11.3 0.0 copy-start.6
  11.4 0.6 copy-done.6
  12.0 0.0 copy-done.2
  12.0 1.1 fusion.4
  13.1 2.1 copy.16
  15.2 10.1 all-to-all-start
  25.3 0.0 all-reduce.7.cloned.1.call-start
  25.3 0.0 copy-done.8
  25.4 102.4 %all_gather.12 = bf16[5120,96]{1,0:T(8,128)(2,1)} all-gather(bf16[80,96]{1,0:T(8,128)(2,1)S(1)} %copy-done.8), channel_id=1, replica_groups=mesh['exp'=8,'rows'=64] {'rows'}, dimensions={0}, use_global_device_ids=true | all-gather | bytes 998400 | tf_op jit(solution)/shard_map/all_gather | solution.py:28
  127.7 0.0 all-to-all-done
  127.7 1.2 convert_reduce_fusion.1
  128.9 0.0 copy-done.3
  128.9 0.0 copy-start.7
  128.9 2.5 fusion.10
  131.4 43.7 %all_gather.14 = bf16[320,768]{0,1:T(8,128)(2,1)S(1)} all-gather(bf16[320,96]{0,1:T(8,128)(2,1)S(1)} %fusion.10), channel_id=1, replica_groups=mesh['exp'=8,'rows'=64] {'exp'}, dimensions={1}, use_global_device_ids=true | all-gather | bytes 552960 | tf_op jit(solution)/shard_map/all_gather | solution.py:42
  175.1 0.8 copy-done.1
  175.9 0.0 copy-done.7
  175.9 1.0 convolution_multiply_fusion.7
  176.9 3.1 fusion.3
  180.0 0.0 all-reduce.7.cloned.1.call-update
  180.0 0.0 reduce-scatter.7.cloned.1.call-start
  180.1 2.1 fusion.1
  182.2 3.1 copy.20
  185.3 0.0 reduce-scatter.7.cloned.1.call-update
  185.4 538.3 %all-reduce.7.cloned.1.call-done = (f32[5120,64]{0,1:T(8,128)}, f32[64,768]{1,0:T(8,128)}) async-done(((f32[5120,64]{0,1:T(8,128)}, f32[64,768]{1,0:T(8,128)}), (f32[5120,64]{0,1:T(8,128)}, f32[64,768]{1,0:T(8,128)})) %all-reduce.7.cloned.1.call-update) | async-done | bytes 1507344 | tf_op jit(solution)/shard_map/psum | solution.py:69
  723.7 1.0 subtract_convert_fusion.3
  724.7 2.6 fusion.21
  727.3 0.0 copy-start.4
  727.3 0.0 copy-start.9
  727.3 1.1 fusion.5
  728.4 2.1 copy.18
  730.5 6.6 all-to-all-start.1
  737.1 0.0 all-reduce.5.cloned.1.call-start
  737.1 0.0 copy-done.9
  737.2 0.1 copy.15
  737.3 11.9 all-to-all-done.1
  749.1 1.8 convert_reduce_fusion
  751.0 257.3 %reduce-scatter.7.cloned.1.call-done = f32[80,96]{1,0:T(8,128)} async-done(((f32[5120,96]{1,0:T(8,128)}), f32[80,96]{1,0:T(8,128)}) %reduce-scatter.7.cloned.1.call-update) | async-done | bytes 30736
  1008.3 1.5 copy.21
  1009.8 0.8 subtract_convert_fusion.5
  1010.6 0.1 copy.17
  1010.7 0.0 copy-done.4
  1010.7 85.1 %all_gather.13 = bf16[5120,96]{1,0:T(8,128)(2,1)S(1)} all-gather(bf16[80,96]{1,0:T(8,128)(2,1)S(1)} %copy.17), channel_id=1, replica_groups=mesh['exp'=8,'rows'=64] {'rows'}, dimensions={0}, use_global_device_ids=true | all-gather | bytes 998400 | tf_op jit(solution)/shard_map/all_gather | solution.py:28
  1095.8 2.2 fusion.16
  1097.9 44.7 %all_gather.15 = bf16[320,768]{0,1:T(8,128)(2,1)} all-gather(bf16[320,96]{0,1:T(8,128)(2,1)S(1)} %fusion.16), channel_id=1, replica_groups=mesh['exp'=8,'rows'=64] {'exp'}, dimensions={1}, use_global_device_ids=true | all-gather | bytes 552960 | tf_op jit(solution)/shard_map/all_gather | solution.py:42
  1142.7 3.1 fusion.2
  1145.8 0.0 copy-done.5
  1145.8 2.1 convolution_multiply_fusion.6
  1147.9 0.0 all-reduce.5.cloned.1.call-update
  1147.9 0.0 reduce-scatter.9.cloned.1.call-start
  1147.9 2.1 fusion
  1150.1 3.1 copy.22
  1153.2 0.0 reduce-scatter.9.cloned.1.call-update
  1153.2 533.9 %all-reduce.5.cloned.1.call-done = (f32[5120,64]{0,1:T(8,128)}, f32[64,768]{1,0:T(8,128)}) async-done(((f32[5120,64]{0,1:T(8,128)}, f32[64,768]{1,0:T(8,128)}), (f32[5120,64]{0,1:T(8,128)}, f32[64,768]{1,0:T(8,128)})) %all-reduce.5.cloned.1.call-update) | async-done | bytes 1507344 | tf_op jit(solution)/shard_map/psum | solution.py:69
  1687.1 1.6 fusion.31
  1688.7 3.0 fusion.23
  1691.7 278.9 %reduce-scatter.9.cloned.1.call-done = f32[80,96]{1,0:T(8,128)} async-done(((f32[5120,96]{1,0:T(8,128)}), f32[80,96]{1,0:T(8,128)}) %reduce-scatter.9.cloned.1.call-update) | async-done | bytes 30736
  1970.6 0.9 copy.23
  1971.4 0.7 copy.19
  (5 shorter events, 0.0 us)
Async XLA Ops:
  7.2 1.9 copy-start
  9.1 2.9 copy-start.2
  11.3 0.6 copy-start.6
  12.0 13.4 copy-start.8
  13.1 115.9 %copy-start.3 = (bf16[320,96]{0,1:T(8,128)(2,1)S(1)}, bf16[320,96]{0,1:T(8,128)(2,1)}, u32[]{:S(2)}) copy-start(bf16[320,96]{0,1:T(8,128)(2,1)} %param.7) | copy-start | bytes 184324
  15.2 112.6 %all-to-all-start = ((bf16[320,8,96]{0,2,1:T(8,128)(2,1)}), bf16[320,8,96]{0,2,1:T(8,128)(2,1)}, u32[]{:S(2)}, u32[]{:S(2)}) async-start(bf16[320,8,96]{0,2,1:T(8,128)(2,1)} %bitcast.56), calls=%async_computation | async-start | bytes 1179648 | tf_op jit(solution)/shard_map/all_to_all | solution.py:39
  25.3 698.4 %all-reduce.7.cloned.1.call-start = ((), (), s32[]{:S(2)}) async-start(), calls=%async_computation.7 | async-start | bytes 3014656 | tf_op jit(solution)/shard_map/psum | solution.py:69
  128.9 47.0 %copy-start.7 = (bf16[320,64]{0,1:T(8,128)(2,1)S(1)}, bf16[320,64]{0,1:T(8,128)(2,1)}, u32[]{:S(2)}) copy-start(bf16[320,64]{0,1:T(8,128)(2,1)} %copy-done.6) | copy-start | bytes 122884
  175.1 0.8 copy-start.1
  180.0 828.2 %reduce-scatter.7.cloned.1.call-start = ((), (), s32[]{:S(2)}) async-start(), calls=%async_computation.4 | async-start | bytes 2662400
  727.3 283.4 %copy-start.4 = (bf16[64,320]{1,0:T(8,128)(2,1)}, bf16[64,320]{1,0:T(8,128)(2,1)S(1)}, u32[]{:S(2)}) copy-start(bf16[64,320]{1,0:T(8,128)(2,1)S(1)} %fusion.21) | copy-start | bytes 122884
  727.3 9.9 copy-start.9
  730.5 18.7 all-to-all-start.1
  737.1 950.0 %all-reduce.5.cloned.1.call-start = ((), (), s32[]{:S(2)}) async-start(), calls=%async_computation.6 | async-start | bytes 3014656 | tf_op jit(solution)/shard_map/psum | solution.py:69
  1142.7 3.1 copy-start.5
  1147.9 822.7 %reduce-scatter.9.cloned.1.call-start = ((), (), s32[]{:S(2)}) async-start(), calls=%async_computation.5 | async-start | bytes 2662400
Sparse Core Ops, SparseCore 0:
  180.2 543.5 all-reduce.6
  726.7 281.4 reduce-scatter.6
  1148.0 539.0 all-reduce.4
  1690.0 280.4 reduce-scatter.8
where the time goes:
time: 1990 us; the launch traced here: 1980 us
  waiting for transfers between devices  1620 us (81%)
  blocking collectives  276 us (14%)
  matrix products  25.2 us (1%)
    psum x2, waiting for transfers between devices, body(): grad_up, grad_down = lax.psum((grad_up, grad_down), 'rows')  1070 us
    unnamed x6, waiting for transfers between devices  536 us
    all_gather x2, blocking collectives, body(): lax.all_gather(base, 'rows', axis=0, tiled=True)  187 us
    all_gather x2, blocking collectives, body(): resid_full = lax.all_gather(resid_cols, 'exp', axis=1, tiled=True)  88.4 us
  transfers between devices with their start and end apart: 6, of which 5 were waited for; matrix products, arithmetic and copies ran while one was open for 1% of the time, Pallas kernels for 0%

commit v1 on v0

v1 whole, which is shorter than its diff:
```python
import functools
import math

import jax
import jax.numpy as jnp
from jax import lax
from jax.experimental import pallas as pl
from jax.experimental.pallas import tpu as pltpu
from jax.sharding import PartitionSpec as P

ITERS = 2
STEP_RATE = 0.25

X, YH, Z, YL = 4, 2, 8, 4
RANK = 64
LANES = 128

f32, bf16 = jnp.float32, jnp.bfloat16
MESH = pl.DeviceIdType.MESH


def dot(a, b):
    return jnp.dot(a, b, preferred_element_type=f32)


def dot_t(a, b):
    return lax.dot_general(a, b, (((1,), (1,)), ((), ())), preferred_element_type=f32)


class Sizes:
    def __init__(self, tok, width, hid, exp_hidden):
        self.t = tok
        self.dh = width // 2
        self.hc = hid
        self.zh = Z // 2
        self.cw = width // Z
        self.nt = self.cw // LANES
        self.db = width // (Z * YL * 2)
        self.experts = X * YH
        self.el = self.experts * RANK // 2
        self.lb = self.el // LANES
        self.dr = hid // 2
        self.na_base = self.nt * hid
        self.na = self.na_base + self.dr
        step = 16 * YL
        self.na_pad = -(-self.na // step) * step
        self.nb = self.nt * RANK
        self.pa = self.na_pad // YL
        self.pb = self.nb // YL
        assert self.zh == 2 * self.lb and self.pb % 16 == 0 and self.na % 16 == 0


def scratch_of(s):
    zr, zl = Z // 2, Z // 2 - 1
    vm = pltpu.VMEM
    return dict(
        calh=vm((2 * s.t, s.dh), bf16),
        uph=vm((s.dh, RANK), bf16),
        bpad=vm((s.db, LANES), bf16),
        bg=vm((s.cw, LANES), bf16),
        tpad=vm((s.t, LANES), f32),
        d0s=vm((s.experts, s.hc, LANES), bf16),
        d0r=vm((s.experts, s.hc, LANES), bf16),
        a=vm((ITERS + 1, s.zh, s.na_pad, LANES), bf16),
        b=vm((ITERS + 1, s.zh, s.nb, LANES), bf16),
        bo=vm((s.zh, s.nb, LANES), bf16),
        dn=vm((ITERS, 2, s.hc, s.el), bf16),
        dnr=vm((ITERS, s.zh, s.dr, LANES), bf16),
        ga=vm((s.zh, s.na, LANES), f32),
        gb=vm((s.zh, s.nb, LANES), f32),
        asr=vm((ITERS, zr, s.na, LANES), bf16),
        arr=vm((ITERS, zr, s.na, LANES), bf16),
        asl=vm((ITERS, zl, s.na, LANES), bf16),
        arl=vm((ITERS, zl, s.na, LANES), bf16),
        bsr=vm((ITERS, zr, s.nb, LANES), bf16),
        brr=vm((ITERS, zr, s.nb, LANES), bf16),
        bsl=vm((ITERS, zl, s.nb, LANES), bf16),
        brl=vm((ITERS, zl, s.nb, LANES), bf16),
        ya=vm((YL, s.pa, LANES), f32),
        yas=vm((ITERS, YL, s.pa, LANES), bf16),
        yar=vm((ITERS, YL, s.pa, LANES), bf16),
        yb=vm((YL, s.pb, LANES), f32),
        ybs=vm((ITERS, YL, s.pb, LANES), bf16),
        ybr=vm((ITERS, YL, s.pb, LANES), bf16),
        xin_s=vm((ITERS, s.t // 2, LANES), f32),
        xin_r=vm((ITERS, s.t // 2, LANES), f32),
        xb_s=vm((ITERS, s.t, LANES), f32),
        xb_r=vm((ITERS, s.t, LANES), f32),
        e1s=vm((ITERS, 2, s.t // 2, LANES), bf16),
        e1r=vm((ITERS, 2, s.t // 2, LANES), bf16),
        e2s=vm((ITERS, 2, s.t // 2, LANES), bf16),
        e2r=vm((ITERS, 2, X, s.t // 2, LANES), bf16),
        ixs=vm((ITERS, 2, s.t, s.el), bf16),
        ixc=vm((ITERS, 2, s.t, s.el), bf16),
        res=vm((ITERS, 2, s.t, LANES), bf16),
        back=vm((ITERS, 2, s.t, LANES), bf16),
        bfin=vm((s.na_base, LANES), bf16),
        fin=vm((s.cw, LANES), f32),
        dnf=vm((s.experts, 2, s.dr, LANES), bf16),
        local_sem=pltpu.SemaphoreType.DMA((4,)),
    )


def kernel(s, n_sem, calib, target, route, base, up, down, o_base, o_up, o_down, *, send, recv,
           calh, uph, bpad, bg, tpad, d0s, d0r, a, b, bo, dn, dnr, ga, gb, asr, arr, asl, arl,
           bsr, brr, bsl, brl, ya, yas, yar, yb, ybs, ybr, xin_s, xin_r, xb_s, xb_r,
           e1s, e1r, e2s, e2r, ixs, ixc, res, back, bfin, fin, dnf, local_sem):
    t, zh, zr, zl = s.t, s.zh, Z // 2, Z // 2 - 1
    width = 2 * s.dh
    inv_d = 1.0 / math.sqrt(width)
    inv_r = 1.0 / math.sqrt(RANK)
    inv_t = 1.0 / math.sqrt(t * Z * YL * 2)

    e, r = lax.axis_index("exp"), lax.axis_index("rows")
    x, yh = e // YH, e % YH
    c, y, z = r % 2, (r // 2) % YL, r // (2 * YL)
    cz = z // zh
    zi = z % zh
    mine = cz == c
    other_core = cz != c
    row_of = lambda z_, y_, c_: (z_ * YL + y_) * 2 + c_
    partner = (e, row_of(z, y, 1 - c))
    right = (e, row_of((z + 1) % Z, y, c))
    left = (e, row_of((z + Z - 1) % Z, y, c))

    used = [0]
    sends = []

    def slot(n=1):
        used[0] += n
        assert used[0] <= n_sem
        return used[0] - n

    def rcopy(src, dst, ss, rs, dev):
        return pltpu.make_async_remote_copy(
            src_ref=src, dst_ref=dst, send_sem=send.at[ss], recv_sem=recv.at[rs],
            device_id=dev, device_id_type=MESH)

    def push(src, dst, ss, rs, dev, cond=None, like=None):
        rcopy(src, dst, ss, rs, dev).start()
        sends.append((cond, like or (lambda: src), ss))

    def landed(dst, rs):
        rcopy(dst, dst, rs, rs, partner).wait_recv()

    lane = lax.broadcasted_iota(jnp.int32, (t // 2, LANES), 1) < RANK

    def pack(v):
        return jnp.where(lane, v[: t // 2], v[t // 2 :])

    def unpack(v):
        w = pltpu.roll(v, RANK, 1)
        return jnp.concatenate([jnp.where(lane, v, w), jnp.where(lane, w, v)], axis=0)

    own_rows = pl.ds(pl.multiple_of(c * t, t), t)
    oth_rows = pl.ds(pl.multiple_of((1 - c) * t, t), t)
    own_cols = pl.ds(pl.multiple_of(c * s.dh, LANES), s.dh)
    oth_cols = pl.ds(pl.multiple_of((1 - c) * s.dh, LANES), s.dh)
    own_half = pl.ds(pl.multiple_of(c * s.dh, 16), s.dh)
    ld_cal = pltpu.make_async_copy(calib.at[:, own_cols], calh.at[own_rows], local_sem.at[0])
    ld_up = pltpu.make_async_copy(up.at[own_half], uph, local_sem.at[1])
    ld_cal.start()
    ld_up.start()

    bar = pltpu.get_barrier_semaphore()
    peers = [partner, right, left]
    for dy in range(1, YL):
        for c_ in (c, 1 - c):
            peers.append((e, row_of(z, (y + dy) % YL, c_)))
    for de in range(1, s.experts):
        peers.append(((e + de) % s.experts, r))
    for dev in peers:
        pl.semaphore_signal(bar, inc=1, device_id=dev, device_id_type=MESH)
    bpad[...] = jnp.zeros_like(bpad)
    bpad[:, : s.hc] = base[...]
    pl.semaphore_wait(bar, len(peers))

    gather_s, gather_r = slot(YL), slot(2 * YL)
    bg_rows = lambda y_, c_: pl.ds(pl.multiple_of((2 * y_ + c_) * s.db, 16), s.db)
    for dy in range(1, YL):
        push(bpad, bg.at[bg_rows(y, c)], gather_s + dy, gather_r + 2 * y + c,
             (e, row_of(z, (y + dy) % YL, cz)))

    @pl.when(other_core)
    def _():
        push(bpad, bg.at[bg_rows(y, c)], gather_s, gather_r + 2 * y + c, partner, other_core)

    @pl.when(mine)
    def _():
        bg[bg_rows(y, c), :] = bpad[...]

    cal_i = slot()
    push(calib.at[:, oth_cols], calh.at[own_rows], cal_i, cal_i, partner)

    dt = jnp.concatenate([down[...].astype(f32), jnp.zeros_like(down, dtype=f32)], axis=0).T
    for j in range(s.experts):
        d0s[j] = dt[j * s.hc : (j + 1) * s.hc].astype(bf16)
    d0_s, d0_r = slot(s.experts), slot(s.experts)
    for de in range(1, s.experts):
        other = (e + de) % s.experts
        push(d0s.at[other], d0r.at[e], d0_s + de, d0_r + de, (other, r))
    d0r[e] = d0s[e]
    tpad[...] = jnp.zeros_like(tpad)
    tpad[:, : s.hc] = target[...].astype(f32)
    a[0, :, s.na :, :] = jnp.zeros((zh, s.na_pad - s.na, LANES), bf16)

    ld_up.wait()
    for k in range(zh):
        for i in range(s.nt):
            lo = k * s.cw + i * LANES
            tile = uph[lo : lo + LANES, :].astype(f32)
            tile = jnp.concatenate([tile, tile], axis=1).T
            b[0, k, i * RANK : (i + 1) * RANK, :] = tile[:RANK].astype(bf16)

    def ag_maker(buf, v, lo, n):
        ss_r, rs_r = slot(zr), slot(zr)
        ss_l, rs_l = slot(max(zl, 1)), slot(max(zl, 1))
        view = lambda k: buf.at[v, k % zh, pl.ds(lo, n)]
        like = lambda: buf.at[v, 0, pl.ds(lo, n)]

        def step(i):
            k = (z + Z - i) % Z
            on = k // zh == c

            @pl.when(on)
            def _():
                if i > 0:
                    landed(view(k), rs_r + i - 1)
                if i < zr:
                    push(view(k), view(k), ss_r + i, rs_r + i, right, on, like)

            if i <= zl:
                k2 = (z + i) % Z
                on2 = k2 // zh == c

                @pl.when(on2)
                def _():
                    if i > 0:
                        landed(view(k2), rs_l + i - 1)
                    if i < zl:
                        push(view(k2), view(k2), ss_l + i, rs_l + i, left, on2, like)

        return step

    def rs_maker(it, g, sr, rr, sl, rl):
        ss_r, rs_r = slot(zr), slot(zr)
        ss_l, rs_l = slot(zl), slot(zl)

        def step(i):
            d = (z + zr - i) % Z
            on = d // zh == c

            @pl.when(on)
            def _():
                val = g[d % zh]
                if i > 0:
                    landed(rr.at[it, i - 1], rs_r + i - 1)
                    val = val + rr[it, i - 1].astype(f32)
                sr[it, i] = val.astype(bf16)
                push(sr.at[it, i], rr.at[it, i], ss_r + i, rs_r + i, right, on,
                     lambda: sr.at[it, i])

            if i < zl:
                d2 = (z + Z - zl + i) % Z
                on2 = d2 // zh == c

                @pl.when(on2)
                def _():
                    val = g[d2 % zh]
                    if i > 0:
                        landed(rl.at[it, i - 1], rs_l + i - 1)
                        val = val + rl[it, i - 1].astype(f32)
                    sl[it, i] = val.astype(bf16)
                    push(sl.at[it, i], rl.at[it, i], ss_l + i, rs_l + i, left, on2,
                         lambda: sl.at[it, i])

        def total():
            landed(rr.at[it, zr - 1], rs_r + zr - 1)
            landed(rl.at[it, zl - 1], rs_l + zl - 1)
            return g[zi] + rr[it, zr - 1].astype(f32) + rl[it, zl - 1].astype(f32)

        return step, total

    def y_maker(it, total, buf, full, send_buf, recv_buf, piece):
        s1, r1 = slot(YL), slot(YL)
        s2, r2 = slot(YL), slot(YL)
        rows = lambda y_: pl.ds(pl.multiple_of(y_ * piece, 16), piece)

        def first():
            @pl.when(mine)
            def _():
                val = total()
                gap = YL * piece - val.shape[0]
                if gap:
                    val = jnp.concatenate([val, jnp.zeros((gap, LANES), f32)], axis=0)
                val = val.reshape(YL, piece, LANES)
                full[...] = val
                send_buf[it] = val.astype(bf16)
                for dy in range(1, YL):
                    o = (y + dy) % YL
                    push(send_buf.at[it, o], recv_buf.at[it, y], s1 + dy, r1 + dy,
                         (e, row_of(z, o, c)), mine, lambda: send_buf.at[it, 0])

        def second():
            @pl.when(mine)
            def _():
                val = full[y]
                for dy in range(1, YL):
                    o = (y + YL - dy) % YL
                    landed(recv_buf.at[it, o], r1 + dy)
                    val = val + recv_buf[it, o].astype(f32)
                old = buf[it, zi, rows(y), :].astype(f32)
                buf[it + 1, zi, rows(y), :] = (old - STEP_RATE * val).astype(bf16)
                for dy in range(1, YL):
                    push(buf.at[it + 1, zi, rows(y)], buf.at[it + 1, zi, rows(y)], s2 + dy,
                         r2 + dy, (e, row_of(z, (y + dy) % YL, c)), mine,
                         lambda: buf.at[it + 1, 0, pl.ds(0, piece)])

        def third():
            @pl.when(mine)
            def _():
                for dy in range(1, YL):
                    landed(buf.at[it + 1, zi, rows((y + YL - dy) % YL)], r2 + dy)

        return first, second, third

    def exp_maker(it, w):
        i1, s2, r2 = slot(), slot(X), slot(X)
        peer = (x * YH + 1 - yh, r)

        def first(val):
            e1s[it, w] = val.astype(bf16)
            push(e1s.at[it, w], e1r.at[it, w], i1, i1, peer)

        def second():
            landed(e1r.at[it, w], i1)
            e2s[it, w] = (e1s[it, w].astype(f32) + e1r[it, w].astype(f32)).astype(bf16)
            for dx in range(1, X):
                push(e2s.at[it, w], e2r.at[it, w, dx], s2 + dx, r2 + dx,
                     (((x + dx) % X) * YH + yh, r))

        def third():
            val = e2s[it, w].astype(f32)
            for dx in range(1, X):
                landed(e2r.at[it, w, dx], r2 + dx)
                val = val + e2r[it, w, dx].astype(f32)
            return val

        return first, second, third

    @pl.when(mine)
    def _():
        for y_ in range(YL):
            for c_ in range(2):
                @pl.when(jnp.logical_not(jnp.logical_and(y_ == y, c_ == c)))
                def _():
                    landed(bg.at[bg_rows(y_, c_)], gather_r + 2 * y_ + c_)
        for i in range(s.nt):
            tile = bg[i * LANES : (i + 1) * LANES, :].astype(f32).T
            a[0, zi, i * s.hc : (i + 1) * s.hc, :] = tile[: s.hc].astype(bf16)

    ag_a = ag_maker(a, 0, 0, s.na_base)
    ag_a(0)
    ag_b = None
    ld_cal.wait()
    mask_own = route[...] == e
    pad_rows = LANES - s.hc

    def hot(h):
        grp = lax.broadcasted_iota(jnp.int32, (t, s.el), 1) // RANK + h * (s.experts // 2)
        return route[...] == grp

    for it in range(ITERS):
        in_i = slot()
        upt = jnp.concatenate(
            [b[it, k, i * RANK : (i + 1) * RANK, :] for k in range(zh) for i in range(s.nt)], axis=1)
        upt = jnp.concatenate([upt, upt], axis=0)
        if it == 0:
            part = dot_t(calh[own_rows, :], upt)
            landed(calh.at[oth_rows], cal_i)
            xin_s[it] = pack(dot_t(calh[oth_rows, :], upt))
            push(xin_s.at[it], xin_r.at[it], in_i, in_i, partner)
        else:
            xin_s[it] = pack(dot_t(calh[oth_rows, :], upt))
            push(xin_s.at[it], xin_r.at[it], in_i, in_i, partner)
            part = dot_t(calh[own_rows, :], upt)
        landed(xin_r.at[it], in_i)
        inner = ((part + unpack(xin_r[it])) * inv_d).astype(bf16).astype(f32)
        inner = jnp.where(mask_own, inner, 0.0)
        x1, x2, x3 = exp_maker(it, 0)
        x1(pack(inner))
        if it == 0:
            ag_a(1)
        x2()
        if it == 0:
            for de in range(1, s.experts):
                landed(d0r.at[(e + s.experts - de) % s.experts], d0_r + de)
            for h in range(2):
                for l in range(s.lb):
                    j = (h * s.lb + l) * 2
                    pair = d0r[j].astype(f32) + pltpu.roll(d0r[j + 1].astype(f32), RANK, 1)
                    dn[0, h, :, l * LANES : (l + 1) * LANES] = pair.astype(bf16)
            for p in range(zh):
                l, h = p // 2, p % 2
                a[0, p, s.na_base : s.na, :] = dn[
                    0, c, h * s.dr : (h + 1) * s.dr, l * LANES : (l + 1) * LANES]
            ag_a(2)
        inner = unpack(x3())
        wide = jnp.concatenate([inner] * s.lb, axis=1)
        for h in range(2):
            ixs[it, h] = jnp.where(hot(h), wide, 0.0).astype(bf16)
        ix_i = slot()
        ixc[it, c] = ixs[it, c]
        push(ixs.at[it, 1 - c], ixc.at[it, c], ix_i, ix_i, partner)
        if it == 0:
            for i in range(3, zr + 1):
                ag_a(i)
        else:
            ag_a(zr)
            dn_i = slot()
            push(a.at[it, :, pl.ds(s.na_base, s.dr)], dnr.at[it], dn_i, dn_i, partner)
        bt = jnp.concatenate(
            [a[it, k, i * s.hc : (i + 1) * s.hc, :] for k in range(zh) for i in range(s.nt)], axis=1)
        if pad_rows:
            bt = jnp.concatenate([bt, jnp.zeros((pad_rows, s.dh), bf16)], axis=0)
        xb_i = slot()
        xb_s[it] = dot_t(calh[oth_rows, :], bt)
        push(xb_s.at[it], xb_r.at[it], xb_i, xb_i, partner)
        part = dot_t(calh[own_rows, :], bt)
        if it > 0:
            landed(dnr.at[it], dn_i)
            for p in range(zh):
                l, h = p // 2, p % 2
                at = (slice(h * s.dr, (h + 1) * s.dr), slice(l * LANES, (l + 1) * LANES))
                dn[(it, c) + at] = a[it, p, s.na_base : s.na, :]
                dn[(it, 1 - c) + at] = dnr[it, p]
        dnw = [dn[it, h] for h in range(2)]
        if pad_rows:
            dnw = [jnp.concatenate([w, jnp.zeros((pad_rows, s.el), bf16)], axis=0) for w in dnw]
        delta = dot_t(ixs[it, 0], dnw[0]) + dot_t(ixs[it, 1], dnw[1])
        delta = (delta * inv_r).astype(bf16).astype(f32)
        landed(xb_r.at[it], xb_i)
        cols = ((part + xb_r[it]) * inv_d).astype(bf16).astype(f32)
        resid = (cols + delta - tpad[...]).astype(bf16)
        res[it, c] = resid
        re_i = slot()
        push(res.at[it, c], res.at[it, c], re_i, re_i, partner)

        fold = jnp.zeros((t, LANES), f32)
        for h in range(2):
            share = jnp.where(hot(h), dot(resid, dnw[h]), 0.0)
            for l in range(s.lb):
                fold = fold + share[:, l * LANES : (l + 1) * LANES]
        fold = (fold + pltpu.roll(fold, RANK, 1)) * inv_r
        b1, b2, b3 = exp_maker(it, 1)
        b1(pack(fold))

        landed(res.at[it, 1 - c], re_i)
        rt = jnp.concatenate([res[it, 0], res[it, 1]], axis=0).astype(f32).T[: s.hc].astype(bf16)
        grad = dot(rt, calh[...]) * inv_t
        for k in range(zh):
            for i in range(s.nt):
                lo = k * s.cw + i * LANES
                ga[k, i * s.hc : (i + 1) * s.hc, :] = grad[:, lo : lo + LANES]
        landed(ixc.at[it, 1 - c], ix_i)
        grad = dot(rt, jnp.concatenate([ixc[it, 0], ixc[it, 1]], axis=0)) * inv_t
        for p in range(zh):
            l, h = p // 2, p % 2
            ga[p, s.na_base : s.na, :] = grad[
                h * s.dr : (h + 1) * s.dr, l * LANES : (l + 1) * LANES]
        rs_a, tot_a = rs_maker(it, ga, asr, arr, asl, arl)
        rs_a(0)
        b2()
        rs_a(1)
        bk = unpack(b3()).astype(bf16).astype(f32)
        back[it, c] = jnp.where(mask_own, bk, 0.0).astype(bf16)
        bk_i = slot()
        push(back.at[it, c], back.at[it, c], bk_i, bk_i, partner)
        landed(back.at[it, 1 - c], bk_i)
        bt = jnp.concatenate([back[it, 0], back[it, 1]], axis=0).astype(f32).T[:RANK].astype(bf16)
        grad = dot(bt, calh[...]) * inv_t
        for k in range(zh):
            for i in range(s.nt):
                lo = k * s.cw + i * LANES
                gb[k, i * RANK : (i + 1) * RANK, :] = grad[:, lo : lo + LANES]
        rs_b, tot_b = rs_maker(it, gb, bsr, brr, bsl, brl)
        rs_b(0)
        for i in range(2, zr):
            rs_a(i)
            rs_b(i - 1)
        ya1, ya2, ya3 = y_maker(it, tot_a, a, ya, yas, yar, s.pa)
        yb1, yb2, yb3 = y_maker(it, tot_b, b, yb, ybs, ybr, s.pb)
        ya1()
        rs_b(zr - 1)
        ya2()
        yb1()
        ya3()
        last = it == ITERS - 1
        ag_b = ag_maker(b, it + 1, 0, s.nb)
        ag_a = ag_maker(a, it + 1, s.na_base, s.dr) if last else ag_maker(a, it + 1, 0, s.na)
        if last:
            bf_i = slot()

            @pl.when(mine)
            def _():
                push(a.at[it + 1, zi, pl.ds(0, s.na_base)], bfin, bf_i, bf_i, partner, mine,
                     lambda: bfin)
                bfin[...] = a[it + 1, zi, : s.na_base, :]

        ag_a(0)
        yb2()
        yb3()
        ag_b(0)
        for i in range(1, zr):
            ag_a(i)
            ag_b(i)
        if not last:
            ag_b(zr)
        else:
            ag_a(zr)

    fs, fr, fc = slot(2 * s.lb), slot(s.experts), slot()
    for l in range(s.lb):
        for h in range(YH):
            other = (s.lb * c + l) * YH + h
            away = other != e
            src = a.at[ITERS, pl.ds(2 * l, 2), pl.ds(s.na_base, s.dr)]

            @pl.when(away)
            def _():
                push(src, dnf.at[e], fs + 2 * l + h, fr + e, (other, r), away, lambda: a.at[ITERS, pl.ds(0, 2), pl.ds(s.na_base, s.dr)])

            @pl.when(other == e)
            def _():
                dnf[e] = a[ITERS, 2 * l : 2 * l + 2, s.na_base : s.na, :]

    @pl.when(other_core)
    def _():
        landed(bfin, bf_i)

    for i in range(s.nt):
        tile = bfin[i * s.hc : (i + 1) * s.hc, :].astype(f32)
        if pad_rows:
            tile = jnp.concatenate([tile, jnp.zeros((pad_rows, LANES), f32)], axis=0)
        fin[i * LANES : (i + 1) * LANES, :] = tile.T
    rows = pl.ds(pl.multiple_of((2 * y + c) * s.db, 16), s.db)
    o_base[...] = fin[rows, :][:, : s.hc].astype(bf16)

    owner = x // s.lb == c

    @pl.when(owner)
    def _():
        for j in range(s.experts):
            @pl.when(j != e)
            def _():
                landed(dnf.at[j], fr + j)
        push(dnf, dnf, fc, fc, partner, owner)

    ag_b(zr)
    fb = slot()
    push(b.at[ITERS], bo, fb, fb, partner)

    @pl.when(jnp.logical_not(owner))
    def _():
        landed(dnf, fc)

    for j in range(s.experts):
        blk = dnf[j].reshape(s.hc, LANES).astype(f32)
        blk = jnp.where(yh == 0, blk, pltpu.roll(blk, RANK, 1))
        o_down[j * s.hc : (j + 1) * s.hc, :] = blk[:, :RANK].astype(bf16)
    o_up[pl.ds(c * zh, zh)] = b[ITERS]
    landed(bo, fb)
    o_up[pl.ds((1 - c) * zh, zh)] = bo[...]

    for cond, src, ss in sends:
        src = src()
        cp = rcopy(src, src, ss, ss, partner)
        if cond is None:
            cp.wait_send()
        else:
            pl.when(cond)(cp.wait_send)


def body(calib, target, route, base, up_factor, down_factor):
    t, width = calib.shape
    s = Sizes(t, width, base.shape[1], down_factor.shape[2])
    n_sem = 320
    any_spec = pl.BlockSpec(memory_space=pl.ANY)
    vmem = pl.BlockSpec(memory_space=pltpu.VMEM)
    scratch = scratch_of(s)
    scratch["send"] = pltpu.SemaphoreType.DMA((n_sem,))
    scratch["recv"] = pltpu.SemaphoreType.DMA((n_sem,))
    hid = down_factor.shape[2]
    o_base, o_up, o_down = pl.pallas_call(
        functools.partial(kernel, s, n_sem),
        out_shape=(
            jax.ShapeDtypeStruct(base.shape, bf16),
            jax.ShapeDtypeStruct((Z, s.nb, LANES), bf16),
            jax.ShapeDtypeStruct((hid, RANK), bf16),
        ),
        in_specs=[any_spec, vmem, vmem, vmem, any_spec, vmem],
        out_specs=(vmem, vmem, vmem),
        scratch_shapes=scratch,
        compiler_params=pltpu.CompilerParams(
            collective_id=0, has_side_effects=True, vmem_limit_bytes=56 * 1024 * 1024
        ),
        name="refine",
    )(calib, target, route[:, None], base, up_factor[0], down_factor[0])
    new_up = o_up.reshape(Z, s.nt, RANK, LANES).transpose(0, 1, 3, 2).reshape(1, width, RANK)
    return o_base, new_up, o_down.T[None]


def solution(mesh):
    in_specs = (
        P("rows", None),
        P("rows", "exp"),
        P("rows"),
        P("rows", "exp"),
        P("exp", None, None),
        P("exp", None, None),
    )
    out_specs = (P("rows", "exp"), P("exp", None, None), P("exp", None, None))
    return jax.shard_map(body, mesh=mesh, in_specs=in_specs, out_specs=out_specs, check_vma=False)
```

time: 1990 us -> 179 us (0.09)
  waiting for transfers between devices: 1620 us -> 0 us
  blocking collectives: 276 us -> 0 us
  Pallas kernels: 0 us -> 167 us
  matrix products: 25.2 us -> 0 us
    psum x2 -> x0, waiting for transfers between devices: 1070 us -> none  [body(): grad_up, grad_down = lax.psum((grad_up, grad_down), 'rows')]
    unnamed x6 -> x0, waiting for transfers between devices: 536 us -> none
    all_gather x4 -> x0, blocking collectives: 276 us -> none  [the longest x2 187 us: body(): lax.all_gather(base, 'rows', axis=0, tiled=True)]
    pallas_call x0 -> x1, Pallas kernels: none -> 167 us  [body(): pl.pallas_call(functools.partial(kernel, s, n_sem), out_shape=(jax.ShapeD...]
    dot_general x12 -> x0, matrix products: 25.2 us -> none  [the longest x2 6.25 us: body(): lax.dot_general(calib, back, (((0,), (0,)), ((), ())), preferred_element_...]
  transfers between devices with their start and end apart: 6 -> 0, of which waited for: 5 -> 0; matrix products, arithmetic and copies ran while one was open for 1% -> 0% of each run, Pallas kernels for 0% -> 0%
where the time goes in v1:
time: 179 us
  Pallas kernels  167 us (93%)
  local copies, waits for them, and re-layouts  10.8 us (6%)
    pallas_call x1, Pallas kernels, body(): pl.pallas_call(functools.partial(kernel, s, n_sem), out_shape=(jax.ShapeD...  167 us
    unnamed x6, local copies, waits for them, and re-layouts  6.25 us

profile of v1, /device:TPU:1, one launch (start us, length us, event | category | flops | bytes accessed | tf_op | source)
XLA Modules:
  0.0 178.7 jit_solution(9612383888647248082)
XLA Ops:
  0.6 1.6 copy.14.target
  2.3 1.5 broadcast_in_dim.8.route
  3.7 2.3 %copy.13 = bf16[1,5120,64]{2,1,0:T(8,128)(2,1)} copy(bf16[1,5120,64]{1,2,0:T(8,128)(2,1)} %param.10) | data formatting | bytes 1310720 | tf_op args[4]
  6.0 167.3 %refine.1 = (bf16[80,96]{1,0:T(8,128)(2,1)}, bf16[8,320,128]{2,1,0:T(8,128)(2,1)}, bf16[768,64]{1,0:T(8,128)(2,1)}) custom-call(bf16[320,5120]{1,0:T(8,128)(2,1)} %calib.1, bf16[320,96]{1,0:T(8,128)(2,1)} %copy.14.target, s32[320,1]{1,0:T(8,128)} %broadcast_in_dim.8.route, bf16[80,96]{1,0:T(8,128)(2,1)} %base.1, bf16[5120,64]{1,0:T(8,128)(2,1)} %bitcast.11, ...), custom_call_target="tpu_custom_call" | custom-call | tf_op jit(solution)/shard_map/refine/pallas_call | solution.py:594
  173.3 0.0 copy-start
  173.3 1.7 copy.17
  175.0 1.6 copy.19
  176.6 1.6 reshape.13
  178.1 0.0 copy-done
  178.1 0.6 copy.21
Async XLA Ops:
  173.3 4.8 %copy-start = (bf16[80,96]{1,0:T(8,128)(2,1)S(1)}, bf16[80,96]{1,0:T(8,128)(2,1)}, u32[]{:S(2)}) copy-start(bf16[80,96]{1,0:T(8,128)(2,1)} %get-tuple-element.18) | copy-start | bytes 46084

commit v2 on v1

--- a/solution.py
+++ b/solution.py
@@ -44,9 +44,9 @@
         self.na = self.na_base + self.dr
         step = 16 * YL
         self.na_pad = -(-self.na // step) * step
-        self.nb = self.nt * RANK
         self.pa = self.na_pad // YL
-        self.pb = self.nb // YL
+        self.pb = RANK // YL
+        self.tp = -(-tok // LANES) * LANES
         assert self.zh == 2 * self.lb and self.pb % 16 == 0 and self.na % 16 == 0
 
 
@@ -55,33 +55,33 @@
     vm = pltpu.VMEM
     return dict(
         calh=vm((2 * s.t, s.dh), bf16),
-        uph=vm((s.dh, RANK), bf16),
+        uph=vm((RANK, s.dh), bf16),
+        tgt=vm((s.hc, s.t), bf16),
+        rou=vm((1, s.t), jnp.int32),
+        bas=vm((s.db, s.hc), bf16),
+        dwn=vm((RANK, s.experts * s.hc), bf16),
         bpad=vm((s.db, LANES), bf16),
         bg=vm((s.cw, LANES), bf16),
-        tpad=vm((s.t, LANES), f32),
+        tpad=vm((LANES, s.tp), f32),
+        tcol=vm((s.t, LANES), f32),
+        rcol=vm((s.t, LANES), f32),
         d0s=vm((s.experts, s.hc, LANES), bf16),
         d0r=vm((s.experts, s.hc, LANES), bf16),
         a=vm((ITERS + 1, s.zh, s.na_pad, LANES), bf16),
-        b=vm((ITERS + 1, s.zh, s.nb, LANES), bf16),
-        bo=vm((s.zh, s.nb, LANES), bf16),
+        b=vm((ITERS + 1, s.zh, RANK, s.cw), bf16),
+        bo=vm((s.zh, RANK, s.cw), bf16),
         dn=vm((ITERS, 2, s.hc, s.el), bf16),
         dnr=vm((ITERS, s.zh, s.dr, LANES), bf16),
         ga=vm((s.zh, s.na, LANES), f32),
-        gb=vm((s.zh, s.nb, LANES), f32),
+        gb=vm((ITERS, s.zh, RANK, s.cw), bf16),
+        gbr=vm((ITERS, Z * YL, s.pb, s.cw), bf16),
         asr=vm((ITERS, zr, s.na, LANES), bf16),
         arr=vm((ITERS, zr, s.na, LANES), bf16),
         asl=vm((ITERS, zl, s.na, LANES), bf16),
         arl=vm((ITERS, zl, s.na, LANES), bf16),
-        bsr=vm((ITERS, zr, s.nb, LANES), bf16),
-        brr=vm((ITERS, zr, s.nb, LANES), bf16),
-        bsl=vm((ITERS, zl, s.nb, LANES), bf16),
-        brl=vm((ITERS, zl, s.nb, LANES), bf16),
         ya=vm((YL, s.pa, LANES), f32),
         yas=vm((ITERS, YL, s.pa, LANES), bf16),
         yar=vm((ITERS, YL, s.pa, LANES), bf16),
-        yb=vm((YL, s.pb, LANES), f32),
-        ybs=vm((ITERS, YL, s.pb, LANES), bf16),
-        ybr=vm((ITERS, YL, s.pb, LANES), bf16),
         xin_s=vm((ITERS, s.t // 2, LANES), f32),
         xin_r=vm((ITERS, s.t // 2, LANES), f32),
         xb_s=vm((ITERS, s.t, LANES), f32),
@@ -97,14 +97,15 @@
         bfin=vm((s.na_base, LANES), bf16),
         fin=vm((s.cw, LANES), f32),
         dnf=vm((s.experts, 2, s.dr, LANES), bf16),
-        local_sem=pltpu.SemaphoreType.DMA((4,)),
+        fdn=vm((s.experts * s.hc, LANES), f32),
+        local_sem=pltpu.SemaphoreType.DMA((6,)),
     )
 
 
 def kernel(s, n_sem, calib, target, route, base, up, down, o_base, o_up, o_down, *, send, recv,
-           calh, uph, bpad, bg, tpad, d0s, d0r, a, b, bo, dn, dnr, ga, gb, asr, arr, asl, arl,
-           bsr, brr, bsl, brl, ya, yas, yar, yb, ybs, ybr, xin_s, xin_r, xb_s, xb_r,
-           e1s, e1r, e2s, e2r, ixs, ixc, res, back, bfin, fin, dnf, local_sem):
+           calh, uph, tgt, rou, bas, dwn, bpad, bg, tpad, tcol, rcol, d0s, d0r, a, b, bo, dn, dnr,
+           ga, gb, gbr, asr, arr, asl, arl, ya, yas, yar, xin_s, xin_r, xb_s, xb_r,
+           e1s, e1r, e2s, e2r, ixs, ixc, res, back, bfin, fin, dnf, fdn, local_sem):
     t, zh, zr, zl = s.t, s.zh, Z // 2, Z // 2 - 1
     width = 2 * s.dh
     inv_d = 1.0 / math.sqrt(width)
@@ -156,14 +157,17 @@
     oth_rows = pl.ds(pl.multiple_of((1 - c) * t, t), t)
     own_cols = pl.ds(pl.multiple_of(c * s.dh, LANES), s.dh)
     oth_cols = pl.ds(pl.multiple_of((1 - c) * s.dh, LANES), s.dh)
-    own_half = pl.ds(pl.multiple_of(c * s.dh, 16), s.dh)
-    ld_cal = pltpu.make_async_copy(calib.at[:, own_cols], calh.at[own_rows], local_sem.at[0])
-    ld_up = pltpu.make_async_copy(up.at[own_half], uph, local_sem.at[1])
-    ld_cal.start()
-    ld_up.start()
+    ld_cal, ld_up, ld_tgt, ld_rou, ld_bas, ld_dwn = [
+        pltpu.make_async_copy(src, dst, local_sem.at[i]) for i, (src, dst) in enumerate((
+            (calib.at[:, own_cols], calh.at[own_rows]), (up.at[:, own_cols], uph), (target, tgt),
+            (route, rou), (base, bas), (down, dwn)))]
+    for ld in (ld_bas, ld_dwn, ld_cal, ld_up, ld_tgt, ld_rou):
+        ld.start()
 
     bar = pltpu.get_barrier_semaphore()
-    peers = [partner, right, left]
+    peers = [partner]
+    for dz in range(1, Z):
+        peers.append((e, row_of((z + dz) % Z, y, c)))
     for dy in range(1, YL):
         for c_ in (c, 1 - c):
             peers.append((e, row_of(z, (y + dy) % YL, c_)))
@@ -172,7 +176,12 @@
     for dev in peers:
         pl.semaphore_signal(bar, inc=1, device_id=dev, device_id_type=MESH)
     bpad[...] = jnp.zeros_like(bpad)
-    bpad[:, : s.hc] = base[...]
+    ld_bas.wait()
+    bpad[:, : s.hc] = bas[...]
+    ld_dwn.wait()
+    dt = jnp.concatenate([dwn[...].astype(f32), jnp.zeros_like(dwn, dtype=f32)], axis=0).T
+    for j in range(s.experts):
+        d0s[j] = dt[j * s.hc : (j + 1) * s.hc].astype(bf16)
     pl.semaphore_wait(bar, len(peers))
 
     gather_s, gather_r = slot(YL), slot(2 * YL)
@@ -192,25 +201,23 @@
     cal_i = slot()
     push(calib.at[:, oth_cols], calh.at[own_rows], cal_i, cal_i, partner)
 
-    dt = jnp.concatenate([down[...].astype(f32), jnp.zeros_like(down, dtype=f32)], axis=0).T
-    for j in range(s.experts):
-        d0s[j] = dt[j * s.hc : (j + 1) * s.hc].astype(bf16)
     d0_s, d0_r = slot(s.experts), slot(s.experts)
     for de in range(1, s.experts):
         other = (e + de) % s.experts
         push(d0s.at[other], d0r.at[e], d0_s + de, d0_r + de, (other, r))
     d0r[e] = d0s[e]
-    tpad[...] = jnp.zeros_like(tpad)
-    tpad[:, : s.hc] = target[...].astype(f32)
     a[0, :, s.na :, :] = jnp.zeros((zh, s.na_pad - s.na, LANES), bf16)
 
     ld_up.wait()
     for k in range(zh):
-        for i in range(s.nt):
-            lo = k * s.cw + i * LANES
-            tile = uph[lo : lo + LANES, :].astype(f32)
-            tile = jnp.concatenate([tile, tile], axis=1).T
-            b[0, k, i * RANK : (i + 1) * RANK, :] = tile[:RANK].astype(bf16)
+        b[0, k] = uph[:, k * s.cw : (k + 1) * s.cw]
+    tpad[...] = jnp.zeros_like(tpad)
+    ld_tgt.wait()
+    tpad[: s.hc, : s.t] = tgt[...].astype(f32)
+    tcol[...] = tpad[...].T[: s.t]
+    ld_rou.wait()
+    tpad[:, : s.t] = jnp.broadcast_to(rou[...].astype(f32), (LANES, s.t))
+    rcol[...] = tpad[...].T[: s.t]
 
     def ag_maker(buf, v, lo, n):
         ss_r, rs_r = slot(zr), slot(zr)
@@ -218,7 +225,12 @@
         view = lambda k: buf.at[v, k % zh, pl.ds(lo, n)]
         like = lambda: buf.at[v, 0, pl.ds(lo, n)]
 
+        done = set()
+
         def step(i):
+            if i in done:
+                return
+            done.add(i)
             k = (z + Z - i) % Z
             on = k // zh == c
 
@@ -324,6 +336,57 @@
 
         return first, second, third
 
+    far = sorted(range(Z), key=lambda dz: -min(dz, Z - dz))
+    others = [(dz, dy) for dz in far for dy in range(YL) if dz or dy]
+    brow = lambda y_: pl.ds(pl.multiple_of(y_ * s.pb, 16), s.pb)
+    half_pieces = zh * YL
+
+    def b_maker(it):
+        s1, r1, s2, r2 = slot(), slot(), slot(), slot()
+
+        def all_but_own(buf, cnt):
+            return lambda: buf.at[it, pl.ds(1, cnt)]
+
+        def first():
+            for dz, dy in others:
+                z_, y_ = (z + dz) % Z, (y + dy) % YL
+
+                @pl.when(z_ // zh == c)
+                def _():
+                    place = (Z - dz) % Z * YL + (YL - dy) % YL
+                    rcopy(gb.at[it, z_ % zh, brow(y_)], gbr.at[it, place], s1, r1,
+                          (e, row_of(z_, y_, c))).start()
+
+            sends.append((mine, all_but_own(gbr, half_pieces - 1), s1))
+            sends.append((other_core, all_but_own(gbr, half_pieces), s1))
+
+        def second():
+            @pl.when(mine)
+            def _():
+                landed(gbr.at[it, pl.ds(1, Z * YL - 1)], r1)
+                val = gb[it, zi, brow(y), :].astype(f32)
+                for i in range(1, Z * YL):
+                    val = val + gbr[it, i].astype(f32)
+                old = b[it, zi, brow(y), :].astype(f32)
+                b[it + 1, zi, brow(y), :] = (old - STEP_RATE * val).astype(bf16)
+                for dz, dy in others:
+                    piece = b.at[it + 1, zi, brow(y)]
+                    rcopy(piece, piece, s2, r2,
+                          (e, row_of((z + dz) % Z, (y + dy) % YL, c))).start()
+
+            sends.append((mine, all_but_own(gbr, Z * YL - 1), s2))
+
+        def third():
+            @pl.when(mine)
+            def _():
+                landed(gbr.at[it, pl.ds(1, half_pieces - 1)], r2)
+
+            @pl.when(other_core)
+            def _():
+                landed(gbr.at[it, pl.ds(1, half_pieces)], r2)
+
+        return first, second, third
+
     def exp_maker(it, w):
         i1, s2, r2 = slot(), slot(X), slot(X)
         peer = (x * YH + 1 - yh, r)
@@ -359,21 +422,25 @@
             tile = bg[i * LANES : (i + 1) * LANES, :].astype(f32).T
             a[0, zi, i * s.hc : (i + 1) * s.hc, :] = tile[: s.hc].astype(bf16)
 
-    ag_a = ag_maker(a, 0, 0, s.na_base)
-    ag_a(0)
-    ag_b = None
+    a0_s, a0_r = slot(Z), slot(zh)
+    base_of = lambda k: a.at[0, k, pl.ds(0, s.na_base)]
+    for dz in far[:-1]:
+        @pl.when(mine)
+        def _():
+            push(base_of(zi), base_of(zi), a0_s + dz, a0_r + zi, (e, row_of((z + dz) % Z, y, c)),
+                 mine, lambda: base_of(0))
+
     ld_cal.wait()
-    mask_own = route[...] == e
+    mask_own = rcol[...] == e.astype(f32)
     pad_rows = LANES - s.hc
 
     def hot(h):
         grp = lax.broadcasted_iota(jnp.int32, (t, s.el), 1) // RANK + h * (s.experts // 2)
-        return route[...] == grp
+        return jnp.concatenate([rcol[...]] * s.lb, axis=1) == grp.astype(f32)
 
     for it in range(ITERS):
         in_i = slot()
-        upt = jnp.concatenate(
-            [b[it, k, i * RANK : (i + 1) * RANK, :] for k in range(zh) for i in range(s.nt)], axis=1)
+        upt = jnp.concatenate([b[it, k] for k in range(zh)], axis=1)
         upt = jnp.concatenate([upt, upt], axis=0)
         if it == 0:
             part = dot_t(calh[own_rows, :], upt)
@@ -389,8 +456,8 @@
         inner = jnp.where(mask_own, inner, 0.0)
         x1, x2, x3 = exp_maker(it, 0)
         x1(pack(inner))
-        if it == 0:
-            ag_a(1)
+        if it > 0:
+            ag_a(zr - 2)
         x2()
         if it == 0:
             for de in range(1, s.experts):
@@ -404,7 +471,8 @@
                 l, h = p // 2, p % 2
                 a[0, p, s.na_base : s.na, :] = dn[
                     0, c, h * s.dr : (h + 1) * s.dr, l * LANES : (l + 1) * LANES]
-            ag_a(2)
+        else:
+            ag_a(zr - 1)
         inner = unpack(x3())
         wide = jnp.concatenate([inner] * s.lb, axis=1)
         for h in range(2):
@@ -413,8 +481,10 @@
         ixc[it, c] = ixs[it, c]
         push(ixs.at[it, 1 - c], ixc.at[it, c], ix_i, ix_i, partner)
         if it == 0:
-            for i in range(3, zr + 1):
-                ag_a(i)
+            for k in range(zh):
+                @pl.when(c * zh + k != z)
+                def _():
+                    landed(base_of(k), a0_r + k)
         else:
             ag_a(zr)
             dn_i = slot()
@@ -441,7 +511,7 @@
         delta = (delta * inv_r).astype(bf16).astype(f32)
         landed(xb_r.at[it], xb_i)
         cols = ((part + xb_r[it]) * inv_d).astype(bf16).astype(f32)
-        resid = (cols + delta - tpad[...]).astype(bf16)
+        resid = (cols + delta - tcol[...]).astype(bf16)
         res[it, c] = resid
         re_i = slot()
         push(res.at[it, c], res.at[it, c], re_i, re_i, partner)
@@ -480,24 +550,19 @@
         bt = jnp.concatenate([back[it, 0], back[it, 1]], axis=0).astype(f32).T[:RANK].astype(bf16)
         grad = dot(bt, calh[...]) * inv_t
         for k in range(zh):
-            for i in range(s.nt):
-                lo = k * s.cw + i * LANES
-                gb[k, i * RANK : (i + 1) * RANK, :] = grad[:, lo : lo + LANES]
-        rs_b, tot_b = rs_maker(it, gb, bsr, brr, bsl, brl)
-        rs_b(0)
+            gb[it, k] = grad[:, k * s.cw : (k + 1) * s.cw].astype(bf16)
+        yb1, yb2, yb3 = b_maker(it)
+        yb1()
         for i in range(2, zr):
             rs_a(i)
-            rs_b(i - 1)
         ya1, ya2, ya3 = y_maker(it, tot_a, a, ya, yas, yar, s.pa)
-        yb1, yb2, yb3 = y_maker(it, tot_b, b, yb, ybs, ybr, s.pb)
         ya1()
-        rs_b(zr - 1)
+        yb2()
         ya2()
-        yb1()
         ya3()
         last = it == ITERS - 1
-        ag_b = ag_maker(b, it + 1, 0, s.nb)
         ag_a = ag_maker(a, it + 1, s.na_base, s.dr) if last else ag_maker(a, it + 1, 0, s.na)
+        ag_a(0)
         if last:
             bf_i = slot()
 
@@ -507,17 +572,10 @@
                      lambda: bfin)
                 bfin[...] = a[it + 1, zi, : s.na_base, :]
 
-        ag_a(0)
-        yb2()
-        yb3()
-        ag_b(0)
-        for i in range(1, zr):
+        for i in range(1, zr + 1 if last else max(zr - 2, 1)):
             ag_a(i)
-            ag_b(i)
         if not last:
-            ag_b(zr)
-        else:
-            ag_a(zr)
+            yb3()
 
     fs, fr, fc = slot(2 * s.lb), slot(s.experts), slot()
     for l in range(s.lb):
@@ -556,7 +614,7 @@
                 landed(dnf.at[j], fr + j)
         push(dnf, dnf, fc, fc, partner, owner)
 
-    ag_b(zr)
+    yb3()
     fb = slot()
     push(b.at[ITERS], bo, fb, fb, partner)
 
@@ -567,10 +625,14 @@
     for j in range(s.experts):
         blk = dnf[j].reshape(s.hc, LANES).astype(f32)
         blk = jnp.where(yh == 0, blk, pltpu.roll(blk, RANK, 1))
-        o_down[j * s.hc : (j + 1) * s.hc, :] = blk[:, :RANK].astype(bf16)
-    o_up[pl.ds(c * zh, zh)] = b[ITERS]
+        fdn[j * s.hc : (j + 1) * s.hc, :] = blk
+    o_down[...] = fdn[...].T[:RANK].astype(bf16)
+    up_cols = lambda c_, k: pl.ds(pl.multiple_of(c_ * s.dh + k * s.cw, LANES), s.cw)
+    for k in range(zh):
+        o_up[:, up_cols(c, k)] = b[ITERS, k]
     landed(bo, fb)
-    o_up[pl.ds((1 - c) * zh, zh)] = bo[...]
+    for k in range(zh):
+        o_up[:, up_cols(1 - c, k)] = bo[k]
 
     for cond, src, ss in sends:
         src = src()
@@ -595,19 +657,18 @@
         functools.partial(kernel, s, n_sem),
         out_shape=(
             jax.ShapeDtypeStruct(base.shape, bf16),
-            jax.ShapeDtypeStruct((Z, s.nb, LANES), bf16),
-            jax.ShapeDtypeStruct((hid, RANK), bf16),
+            jax.ShapeDtypeStruct((RANK, width), bf16),
+            jax.ShapeDtypeStruct((RANK, hid), bf16),
         ),
-        in_specs=[any_spec, vmem, vmem, vmem, any_spec, vmem],
+        in_specs=[any_spec] * 6,
         out_specs=(vmem, vmem, vmem),
         scratch_shapes=scratch,
         compiler_params=pltpu.CompilerParams(
             collective_id=0, has_side_effects=True, vmem_limit_bytes=56 * 1024 * 1024
         ),
         name="refine",
-    )(calib, target, route[:, None], base, up_factor[0], down_factor[0])
-    new_up = o_up.reshape(Z, s.nt, RANK, LANES).transpose(0, 1, 3, 2).reshape(1, width, RANK)
-    return o_base, new_up, o_down.T[None]
+    )(calib, target.T, route[None], base, up_factor[0].T, down_factor[0])
+    return o_base, o_up.T[None], o_down[None]
 
 
 def solution(mesh):

time: 179 us -> 173 us (0.966)
  local copies, waits for them, and re-layouts: 10.8 us -> 6.08 us
  Pallas kernels: 167 us -> 165 us
    reshape x2 -> x0, local copies, waits for them, and re-layouts: 3.12 us -> none  [body(): o_up.reshape(Z, s.nt, RANK, LANES).transpose(0, 1, 3, 2)]
    pallas_call x1, Pallas kernels: 167 us -> 165 us  [body(): pl.pallas_call(functools.partial(kernel, s, n_sem), out_shape=(jax.ShapeD...]
    unnamed x6 -> x3, local copies, waits for them, and re-layouts: 6.25 us -> 4.84 us
where the time goes in v2:
time: 173 us; the launch traced here: 171 us
  Pallas kernels  165 us (95%)
  local copies, waits for them, and re-layouts  6.08 us (4%)
    pallas_call x1, Pallas kernels, body(): pl.pallas_call(functools.partial(kernel, s, n_sem), out_shape=(jax.ShapeD...  165 us
    unnamed x3, local copies, waits for them, and re-layouts  4.84 us

profile of v2, /device:TPU:1, one launch (start us, length us, event | category | flops | bytes accessed | tf_op | source)
XLA Modules:
  0.0 171.3 jit_solution(4649007816310936687)
XLA Ops:
  0.6 1.2 broadcast_in_dim.9.route
  1.9 164.6 %refine.1 = (bf16[80,96]{1,0:T(8,128)(2,1)}, bf16[64,5120]{1,0:T(8,128)(2,1)}, bf16[64,768]{1,0:T(8,128)(2,1)}) custom-call(bf16[320,5120]{1,0:T(8,128)(2,1)} %calib.1, bf16[96,320]{1,0:T(8,128)(2,1)} %bitcast.13, s32[1,320]{1,0:T(1,128)} %broadcast_in_dim.9.route, bf16[80,96]{1,0:T(8,128)(2,1)} %base.1, bf16[64,5120]{1,0:T(8,128)(2,1)} %bitcast.9, ...), custom_call_target="tpu_custom_call" | custom-call | tf_op jit(solution)/shard_map/refine/pallas_call | solution.py:656
  166.5 1.3 copy.12
  167.8 2.0 %copy.13 = bf16[1,5120,64]{1,2,0:T(8,128)(2,1)} copy(bf16[1,5120,64]{1,2,0:T(8,128)(2,1)} %bitcast.10) | data formatting | bytes 1310720
  169.8 1.5 copy.14

commit v3 on v2

--- a/solution.py
+++ b/solution.py
@@ -55,6 +55,7 @@
     vm = pltpu.VMEM
     return dict(
         calh=vm((2 * s.t, s.dh), bf16),
+        calo=vm((s.t, s.dh), bf16),
         uph=vm((RANK, s.dh), bf16),
         tgt=vm((s.hc, s.t), bf16),
         rou=vm((1, s.t), jnp.int32),
@@ -72,16 +73,10 @@
         bo=vm((s.zh, RANK, s.cw), bf16),
         dn=vm((ITERS, 2, s.hc, s.el), bf16),
         dnr=vm((ITERS, s.zh, s.dr, LANES), bf16),
-        ga=vm((s.zh, s.na, LANES), f32),
+        ga=vm((ITERS, s.zh, s.na_pad, LANES), bf16),
+        gar=vm((ITERS, Z * YL, s.pa, LANES), bf16),
         gb=vm((ITERS, s.zh, RANK, s.cw), bf16),
         gbr=vm((ITERS, Z * YL, s.pb, s.cw), bf16),
-        asr=vm((ITERS, zr, s.na, LANES), bf16),
-        arr=vm((ITERS, zr, s.na, LANES), bf16),
-        asl=vm((ITERS, zl, s.na, LANES), bf16),
-        arl=vm((ITERS, zl, s.na, LANES), bf16),
-        ya=vm((YL, s.pa, LANES), f32),
-        yas=vm((ITERS, YL, s.pa, LANES), bf16),
-        yar=vm((ITERS, YL, s.pa, LANES), bf16),
         xin_s=vm((ITERS, s.t // 2, LANES), f32),
         xin_r=vm((ITERS, s.t // 2, LANES), f32),
         xb_s=vm((ITERS, s.t, LANES), f32),
@@ -98,13 +93,13 @@
         fin=vm((s.cw, LANES), f32),
         dnf=vm((s.experts, 2, s.dr, LANES), bf16),
         fdn=vm((s.experts * s.hc, LANES), f32),
-        local_sem=pltpu.SemaphoreType.DMA((6,)),
+        local_sem=pltpu.SemaphoreType.DMA((7,)),
     )
 
 
 def kernel(s, n_sem, calib, target, route, base, up, down, o_base, o_up, o_down, *, send, recv,
-           calh, uph, tgt, rou, bas, dwn, bpad, bg, tpad, tcol, rcol, d0s, d0r, a, b, bo, dn, dnr,
-           ga, gb, gbr, asr, arr, asl, arl, ya, yas, yar, xin_s, xin_r, xb_s, xb_r,
+           calh, calo, uph, tgt, rou, bas, dwn, bpad, bg, tpad, tcol, rcol, d0s, d0r, a, b, bo, dn, dnr,
+           ga, gar, gb, gbr, xin_s, xin_r, xb_s, xb_r,
            e1s, e1r, e2s, e2r, ixs, ixc, res, back, bfin, fin, dnf, fdn, local_sem):
     t, zh, zr, zl = s.t, s.zh, Z // 2, Z // 2 - 1
     width = 2 * s.dh
@@ -157,11 +152,11 @@
     oth_rows = pl.ds(pl.multiple_of((1 - c) * t, t), t)
     own_cols = pl.ds(pl.multiple_of(c * s.dh, LANES), s.dh)
     oth_cols = pl.ds(pl.multiple_of((1 - c) * s.dh, LANES), s.dh)
-    ld_cal, ld_up, ld_tgt, ld_rou, ld_bas, ld_dwn = [
+    ld_cal, ld_up, ld_tgt, ld_rou, ld_bas, ld_dwn, ld_oth = [
         pltpu.make_async_copy(src, dst, local_sem.at[i]) for i, (src, dst) in enumerate((
             (calib.at[:, own_cols], calh.at[own_rows]), (up.at[:, own_cols], uph), (target, tgt),
-            (route, rou), (base, bas), (down, dwn)))]
-    for ld in (ld_bas, ld_dwn, ld_cal, ld_up, ld_tgt, ld_rou):
+            (route, rou), (base, bas), (down, dwn), (calib.at[:, oth_cols], calo)))]
+    for ld in (ld_bas, ld_dwn, ld_oth, ld_cal, ld_up, ld_tgt, ld_rou):
         ld.start()
 
     bar = pltpu.get_barrier_semaphore()
@@ -199,7 +194,8 @@
         bg[bg_rows(y, c), :] = bpad[...]
 
     cal_i = slot()
-    push(calib.at[:, oth_cols], calh.at[own_rows], cal_i, cal_i, partner)
+    ld_oth.wait()
+    push(calo, calh.at[own_rows], cal_i, cal_i, partner)
 
     d0_s, d0_r = slot(s.experts), slot(s.experts)
     for de in range(1, s.experts):
@@ -254,136 +250,69 @@
 
         return step
 
-    def rs_maker(it, g, sr, rr, sl, rl):
-        ss_r, rs_r = slot(zr), slot(zr)
-        ss_l, rs_l = slot(zl), slot(zl)
-
-        def step(i):
-            d = (z + zr - i) % Z
-            on = d // zh == c
-
-            @pl.when(on)
-            def _():
-                val = g[d % zh]
-                if i > 0:
-                    landed(rr.at[it, i - 1], rs_r + i - 1)
-                    val = val + rr[it, i - 1].astype(f32)
-                sr[it, i] = val.astype(bf16)
-                push(sr.at[it, i], rr.at[it, i], ss_r + i, rs_r + i, right, on,
-                     lambda: sr.at[it, i])
-
-            if i < zl:
-                d2 = (z + Z - zl + i) % Z
-                on2 = d2 // zh == c
-
-                @pl.when(on2)
-                def _():
-                    val = g[d2 % zh]
-                    if i > 0:
-                        landed(rl.at[it, i - 1], rs_l + i - 1)
-                        val = val + rl[it, i - 1].astype(f32)
-                    sl[it, i] = val.astype(bf16)
-                    push(sl.at[it, i], rl.at[it, i], ss_l + i, rs_l + i, left, on2,
-                         lambda: sl.at[it, i])
-
-        def total():
-            landed(rr.at[it, zr - 1], rs_r + zr - 1)
-            landed(rl.at[it, zl - 1], rs_l + zl - 1)
-            return g[zi] + rr[it, zr - 1].astype(f32) + rl[it, zl - 1].astype(f32)
-
-        return step, total
-
-    def y_maker(it, total, buf, full, send_buf, recv_buf, piece):
-        s1, r1 = slot(YL), slot(YL)
-        s2, r2 = slot(YL), slot(YL)
-        rows = lambda y_: pl.ds(pl.multiple_of(y_ * piece, 16), piece)
+    far = sorted(range(Z), key=lambda dz: -min(dz, Z - dz))
+    others = [(dz, dy) for dz in far for dy in range(YL) if dz or dy]
+    half_pieces = zh * YL
+
+    def sum_maker(it, buf, g, got, size, everywhere):
+        s1, r1, s2, r2 = slot(), slot(), slot(YL), slot(YL)
+        rows = lambda y_: pl.ds(pl.multiple_of(y_ * size, 16), size)
+
+        def some(cnt):
+            return lambda: got.at[it, pl.ds(1, cnt)]
 
         def first():
-            @pl.when(mine)
-            def _():
-                val = total()
-                gap = YL * piece - val.shape[0]
-                if gap:
-                    val = jnp.concatenate([val, jnp.zeros((gap, LANES), f32)], axis=0)
-                val = val.reshape(YL, piece, LANES)
-                full[...] = val
-                send_buf[it] = val.astype(bf16)
-                for dy in range(1, YL):
-                    o = (y + dy) % YL
-                    push(send_buf.at[it, o], recv_buf.at[it, y], s1 + dy, r1 + dy,
-                         (e, row_of(z, o, c)), mine, lambda: send_buf.at[it, 0])
+            for dz, dy in others:
+                z_, y_ = (z + dz) % Z, (y + dy) % YL
+
+                @pl.when(z_ // zh == c)
+                def _():
+                    place = (Z - dz) % Z * YL + (YL - dy) % YL
+                    rcopy(g.at[it, z_ % zh, rows(y_)], got.at[it, place], s1, r1,
+                          (e, row_of(z_, y_, c))).start()
+
+            sends.append((mine, some(half_pieces - 1), s1))
+            sends.append((other_core, some(half_pieces), s1))
 
         def second():
             @pl.when(mine)
             def _():
-                val = full[y]
-                for dy in range(1, YL):
-                    o = (y + YL - dy) % YL
-                    landed(recv_buf.at[it, o], r1 + dy)
-                    val = val + recv_buf[it, o].astype(f32)
+                landed(got.at[it, pl.ds(1, Z * YL - 1)], r1)
+                val = g[it, zi, rows(y), :].astype(f32)
+                for i in range(1, Z * YL):
+                    val = val + got[it, i].astype(f32)
                 old = buf[it, zi, rows(y), :].astype(f32)
                 buf[it + 1, zi, rows(y), :] = (old - STEP_RATE * val).astype(bf16)
+                piece = buf.at[it + 1, zi, rows(y)]
+                if everywhere:
+                    for dz, dy in others:
+                        rcopy(piece, piece, s2, r2,
+                              (e, row_of((z + dz) % Z, (y + dy) % YL, c))).start()
+                else:
+                    for dy in range(1, YL):
+                        rcopy(piece, piece, s2 + dy, r2 + dy,
+                              (e, row_of(z, (y + dy) % YL, c))).start()
+
+            if everywhere:
+                sends.append((mine, some(Z * YL - 1), s2))
+            else:
                 for dy in range(1, YL):
-                    push(buf.at[it + 1, zi, rows(y)], buf.at[it + 1, zi, rows(y)], s2 + dy,
-                         r2 + dy, (e, row_of(z, (y + dy) % YL, c)), mine,
-                         lambda: buf.at[it + 1, 0, pl.ds(0, piece)])
+                    sends.append((mine, lambda: got.at[it, 0], s2 + dy))
 
         def third():
-            @pl.when(mine)
-            def _():
-                for dy in range(1, YL):
-                    landed(buf.at[it + 1, zi, rows((y + YL - dy) % YL)], r2 + dy)
-
-        return first, second, third
-
-    far = sorted(range(Z), key=lambda dz: -min(dz, Z - dz))
-    others = [(dz, dy) for dz in far for dy in range(YL) if dz or dy]
-    brow = lambda y_: pl.ds(pl.multiple_of(y_ * s.pb, 16), s.pb)
-    half_pieces = zh * YL
-
-    def b_maker(it):
-        s1, r1, s2, r2 = slot(), slot(), slot(), slot()
-
-        def all_but_own(buf, cnt):
-            return lambda: buf.at[it, pl.ds(1, cnt)]
-
-        def first():
-            for dz, dy in others:
-                z_, y_ = (z + dz) % Z, (y + dy) % YL
-
-                @pl.when(z_ // zh == c)
-                def _():
-                    place = (Z - dz) % Z * YL + (YL - dy) % YL
-                    rcopy(gb.at[it, z_ % zh, brow(y_)], gbr.at[it, place], s1, r1,
-                          (e, row_of(z_, y_, c))).start()
-
-            sends.append((mine, all_but_own(gbr, half_pieces - 1), s1))
-            sends.append((other_core, all_but_own(gbr, half_pieces), s1))
-
-        def second():
-            @pl.when(mine)
-            def _():
-                landed(gbr.at[it, pl.ds(1, Z * YL - 1)], r1)
-                val = gb[it, zi, brow(y), :].astype(f32)
-                for i in range(1, Z * YL):
-                    val = val + gbr[it, i].astype(f32)
-                old = b[it, zi, brow(y), :].astype(f32)
-                b[it + 1, zi, brow(y), :] = (old - STEP_RATE * val).astype(bf16)
-                for dz, dy in others:
-                    piece = b.at[it + 1, zi, brow(y)]
-                    rcopy(piece, piece, s2, r2,
-                          (e, row_of((z + dz) % Z, (y + dy) % YL, c))).start()
-
-            sends.append((mine, all_but_own(gbr, Z * YL - 1), s2))
-
-        def third():
-            @pl.when(mine)
-            def _():
-                landed(gbr.at[it, pl.ds(1, half_pieces - 1)], r2)
-
-            @pl.when(other_core)
-            def _():
-                landed(gbr.at[it, pl.ds(1, half_pieces)], r2)
+            if everywhere:
+                @pl.when(mine)
+                def _():
+                    landed(got.at[it, pl.ds(1, half_pieces - 1)], r2)
+
+                @pl.when(other_core)
+                def _():
+                    landed(got.at[it, pl.ds(1, half_pieces)], r2)
+            else:
+                @pl.when(mine)
+                def _():
+                    for dy in range(1, YL):
+                        landed(buf.at[it + 1, zi, rows((y + YL - dy) % YL)], r2 + dy)
 
         return first, second, third
 
@@ -531,17 +460,17 @@
         for k in range(zh):
             for i in range(s.nt):
                 lo = k * s.cw + i * LANES
-                ga[k, i * s.hc : (i + 1) * s.hc, :] = grad[:, lo : lo + LANES]
+                ga[it, k, i * s.hc : (i + 1) * s.hc, :] = grad[:, lo : lo + LANES].astype(bf16)
         landed(ixc.at[it, 1 - c], ix_i)
         grad = dot(rt, jnp.concatenate([ixc[it, 0], ixc[it, 1]], axis=0)) * inv_t
         for p in range(zh):
             l, h = p // 2, p % 2
-            ga[p, s.na_base : s.na, :] = grad[
-                h * s.dr : (h + 1) * s.dr, l * LANES : (l + 1) * LANES]
-        rs_a, tot_a = rs_maker(it, ga, asr, arr, asl, arl)
-        rs_a(0)
+            ga[it, p, s.na_base : s.na, :] = grad[
+                h * s.dr : (h + 1) * s.dr, l * LANES : (l + 1) * LANES].astype(bf16)
+        ga[it, :, s.na :, :] = jnp.zeros((zh, s.na_pad - s.na, LANES), bf16)
+        ya1, ya2, ya3 = sum_maker(it, a, ga, gar, s.pa, False)
+        ya1()
         b2()
-        rs_a(1)
         bk = unpack(b3()).astype(bf16).astype(f32)
         back[it, c] = jnp.where(mask_own, bk, 0.0).astype(bf16)
         bk_i = slot()
@@ -551,29 +480,33 @@
         grad = dot(bt, calh[...]) * inv_t
         for k in range(zh):
             gb[it, k] = grad[:, k * s.cw : (k + 1) * s.cw].astype(bf16)
-        yb1, yb2, yb3 = b_maker(it)
+        yb1, yb2, yb3 = sum_maker(it, b, gb, gbr, s.pb, True)
         yb1()
-        for i in range(2, zr):
-            rs_a(i)
-        ya1, ya2, ya3 = y_maker(it, tot_a, a, ya, yas, yar, s.pa)
-        ya1()
+        ya2()
         yb2()
-        ya2()
         ya3()
         last = it == ITERS - 1
-        ag_a = ag_maker(a, it + 1, s.na_base, s.dr) if last else ag_maker(a, it + 1, 0, s.na)
-        ag_a(0)
-        if last:
-            bf_i = slot()
+        if not last:
+            ag_a = ag_maker(a, it + 1, 0, s.na)
+            for i in range(max(zr - 2, 1)):
+                ag_a(i)
+        else:
+            bf_i, dn_s, dn_r = slot(), slot(Z), slot(zh)
+            dn_of = lambda k: a.at[ITERS, k, pl.ds(s.na_base, s.dr)]
 
             @pl.when(mine)
             def _():
-                push(a.at[it + 1, zi, pl.ds(0, s.na_base)], bfin, bf_i, bf_i, partner, mine,
+                for dz in far[:-1]:
+                    push(dn_of(zi), dn_of(zi), dn_s + dz, dn_r + zi,
+                         (e, row_of((z + dz) % Z, y, c)), mine, lambda: dn_of(0))
+                push(a.at[ITERS, zi, pl.ds(0, s.na_base)], bfin, bf_i, bf_i, partner, mine,
                      lambda: bfin)
-                bfin[...] = a[it + 1, zi, : s.na_base, :]
-
-        for i in range(1, zr + 1 if last else max(zr - 2, 1)):
-            ag_a(i)
+                bfin[...] = a[ITERS, zi, : s.na_base, :]
+
+            for k in range(zh):
+                @pl.when(c * zh + k != z)
+                def _():
+                    landed(dn_of(k), dn_r + k)
         if not last:
             yb3()
 

time: 173 us -> 159 us (0.919)
  Pallas kernels: 165 us -> 151 us
    pallas_call x1, Pallas kernels: 165 us -> 151 us  [body(): pl.pallas_call(functools.partial(kernel, s, n_sem), out_shape=(jax.ShapeD...]
where the time goes in v3:
time: 159 us; the launch traced here: 158 us
  Pallas kernels  151 us (95%)
  local copies, waits for them, and re-layouts  6.08 us (4%)
    pallas_call x1, Pallas kernels, body(): pl.pallas_call(functools.partial(kernel, s, n_sem), out_shape=(jax.ShapeD...  151 us
    unnamed x3, local copies, waits for them, and re-layouts  4.84 us

profile of v3, /device:TPU:1, one launch (start us, length us, event | category | flops | bytes accessed | tf_op | source)
XLA Modules:
  0.0 158.2 jit_solution(1240738037329245051)
XLA Ops:
  0.6 1.2 broadcast_in_dim.9.route
  1.9 151.5 %refine.1 = (bf16[80,96]{1,0:T(8,128)(2,1)}, bf16[64,5120]{1,0:T(8,128)(2,1)}, bf16[64,768]{1,0:T(8,128)(2,1)}) custom-call(bf16[320,5120]{1,0:T(8,128)(2,1)} %calib.1, bf16[96,320]{1,0:T(8,128)(2,1)} %bitcast.13, s32[1,320]{1,0:T(1,128)} %broadcast_in_dim.9.route, bf16[80,96]{1,0:T(8,128)(2,1)} %base.1, bf16[64,5120]{1,0:T(8,128)(2,1)} %bitcast.9, ...), custom_call_target="tpu_custom_call" | custom-call | tf_op jit(solution)/shard_map/refine/pallas_call | solution.py:589
  153.4 1.3 copy.12
  154.7 2.0 %copy.13 = bf16[1,5120,64]{1,2,0:T(8,128)(2,1)} copy(bf16[1,5120,64]{1,2,0:T(8,128)(2,1)} %bitcast.10) | data formatting | bytes 1310720
  156.7 1.5 copy.14

commit v4 on v3

--- a/solution.py
+++ b/solution.py
@@ -51,7 +51,6 @@
 
 
 def scratch_of(s):
-    zr, zl = Z // 2, Z // 2 - 1
     vm = pltpu.VMEM
     return dict(
         calh=vm((2 * s.t, s.dh), bf16),
@@ -101,7 +100,7 @@
            calh, calo, uph, tgt, rou, bas, dwn, bpad, bg, tpad, tcol, rcol, d0s, d0r, a, b, bo, dn, dnr,
            ga, gar, gb, gbr, xin_s, xin_r, xb_s, xb_r,
            e1s, e1r, e2s, e2r, ixs, ixc, res, back, bfin, fin, dnf, fdn, local_sem):
-    t, zh, zr, zl = s.t, s.zh, Z // 2, Z // 2 - 1
+    t, zh = s.t, s.zh
     width = 2 * s.dh
     inv_d = 1.0 / math.sqrt(width)
     inv_r = 1.0 / math.sqrt(RANK)
@@ -116,8 +115,6 @@
     other_core = cz != c
     row_of = lambda z_, y_, c_: (z_ * YL + y_) * 2 + c_
     partner = (e, row_of(z, y, 1 - c))
-    right = (e, row_of((z + 1) % Z, y, c))
-    left = (e, row_of((z + Z - 1) % Z, y, c))
 
     used = [0]
     sends = []
@@ -197,11 +194,6 @@
     ld_oth.wait()
     push(calo, calh.at[own_rows], cal_i, cal_i, partner)
 
-    d0_s, d0_r = slot(s.experts), slot(s.experts)
-    for de in range(1, s.experts):
-        other = (e + de) % s.experts
-        push(d0s.at[other], d0r.at[e], d0_s + de, d0_r + de, (other, r))
-    d0r[e] = d0s[e]
     a[0, :, s.na :, :] = jnp.zeros((zh, s.na_pad - s.na, LANES), bf16)
 
     ld_up.wait()
@@ -215,40 +207,50 @@
     tpad[:, : s.t] = jnp.broadcast_to(rou[...].astype(f32), (LANES, s.t))
     rcol[...] = tpad[...].T[: s.t]
 
-    def ag_maker(buf, v, lo, n):
-        ss_r, rs_r = slot(zr), slot(zr)
-        ss_l, rs_l = slot(max(zl, 1)), slot(max(zl, 1))
-        view = lambda k: buf.at[v, k % zh, pl.ds(lo, n)]
-        like = lambda: buf.at[v, 0, pl.ds(lo, n)]
-
-        done = set()
-
-        def step(i):
-            if i in done:
-                return
-            done.add(i)
-            k = (z + Z - i) % Z
-            on = k // zh == c
-
-            @pl.when(on)
-            def _():
-                if i > 0:
-                    landed(view(k), rs_r + i - 1)
-                if i < zr:
-                    push(view(k), view(k), ss_r + i, rs_r + i, right, on, like)
-
-            if i <= zl:
-                k2 = (z + i) % Z
-                on2 = k2 // zh == c
-
-                @pl.when(on2)
+    def ag_maker(buf, v, n):
+        near = Z // 4
+        ss, ss2 = slot(2 * near), slot(2 * near)
+        whole, half_a, half_b = slot(zh), slot(zh), slot(zh)
+        cut = n // 32 * 16
+        view = lambda k, lo=0, m=n: buf.at[v, k % zh, pl.ds(lo, m)]
+        dev = lambda dz: (e, row_of((z + Z + dz) % Z, y, c))
+
+        def first():
+            for q in range(near, 0, -1):
+                for i, sign in enumerate((1, -1)):
+                    push(view(z), view(z), ss + 2 * (q - 1) + i, whole + zi, dev(sign * q), mine,
+                         lambda: view(0))
+
+        def second():
+            for i, sign in enumerate((1, -1)):
+                k = (z + Z - sign * near) % Z
+                on = k // zh == c
+                for q in range(near, 0, -1):
+                    lo, m, rs = (0, n, whole) if q < near else (
+                        (0, cut, half_a) if sign > 0 else (cut, n - cut, half_b))
+
+                    @pl.when(on)
+                    def _():
+                        if q == near:
+                            landed(view(k), whole + k % zh)
+                        push(view(k, lo, m), view(k, lo, m), ss2 + 2 * (q - 1) + i, rs + k % zh,
+                             dev(sign * q), on, lambda lo=lo, m=m: view(0, lo, m))
+
+        def third():
+            for dz in range(1, Z):
+                if dz in (near, Z - near):
+                    continue
+                k = (z + Z - dz) % Z
+
+                @pl.when(k // zh == c)
                 def _():
-                    if i > 0:
-                        landed(view(k2), rs_l + i - 1)
-                    if i < zl:
-                        push(view(k2), view(k2), ss_l + i, rs_l + i, left, on2, like)
-
-        return step
+                    if dz == Z // 2:
+                        landed(view(k, 0, cut), half_a + k % zh)
+                        landed(view(k, cut, n - cut), half_b + k % zh)
+                    else:
+                        landed(view(k), whole + k % zh)
+
+        return first, second, third
 
     far = sorted(range(Z), key=lambda dz: -min(dz, Z - dz))
     others = [(dz, dy) for dz in far for dy in range(YL) if dz or dy]
@@ -351,14 +353,8 @@
             tile = bg[i * LANES : (i + 1) * LANES, :].astype(f32).T
             a[0, zi, i * s.hc : (i + 1) * s.hc, :] = tile[: s.hc].astype(bf16)
 
-    a0_s, a0_r = slot(Z), slot(zh)
-    base_of = lambda k: a.at[0, k, pl.ds(0, s.na_base)]
-    for dz in far[:-1]:
-        @pl.when(mine)
-        def _():
-            push(base_of(zi), base_of(zi), a0_s + dz, a0_r + zi, (e, row_of((z + dz) % Z, y, c)),
-                 mine, lambda: base_of(0))
-
+    ag1, ag2, ag3 = ag_maker(a, 0, s.na_base)
+    pl.when(mine)(ag1)
     ld_cal.wait()
     mask_own = rcol[...] == e.astype(f32)
     pad_rows = LANES - s.hc
@@ -385,9 +381,33 @@
         inner = jnp.where(mask_own, inner, 0.0)
         x1, x2, x3 = exp_maker(it, 0)
         x1(pack(inner))
+        if it == 0:
+            ag2()
+            d0_s, d0_r = slot(s.experts), slot(s.experts)
+            for de in range(1, s.experts):
+                other = (e + de) % s.experts
+                push(d0s.at[other], d0r.at[e], d0_s + de, d0_r + de, (other, r))
+            d0r[e] = d0s[e]
+        x2()
+        ag3()
         if it > 0:
-            ag_a(zr - 2)
-        x2()
+            dn_i = slot()
+            push(a.at[it, :, pl.ds(s.na_base, s.dr)], dnr.at[it], dn_i, dn_i, partner)
+        bt = jnp.concatenate(
+            [a[it, k, i * s.hc : (i + 1) * s.hc, :] for k in range(zh) for i in range(s.nt)], axis=1)
+        if pad_rows:
+            bt = jnp.concatenate([bt, jnp.zeros((pad_rows, s.dh), bf16)], axis=0)
+        xb_i = slot()
+        xb_s[it] = dot_t(calh[oth_rows, :], bt)
+        push(xb_s.at[it], xb_r.at[it], xb_i, xb_i, partner)
+        part = dot_t(calh[own_rows, :], bt)
+        inner = unpack(x3())
+        wide = jnp.concatenate([inner] * s.lb, axis=1)
+        for h in range(2):
+            ixs[it, h] = jnp.where(hot(h), wide, 0.0).astype(bf16)
+        ix_i = slot()
+        ixc[it, c] = ixs[it, c]
+        push(ixs.at[it, 1 - c], ixc.at[it, c], ix_i, ix_i, partner)
         if it == 0:
             for de in range(1, s.experts):
                 landed(d0r.at[(e + s.experts - de) % s.experts], d0_r + de)
@@ -401,32 +421,6 @@
                 a[0, p, s.na_base : s.na, :] = dn[
                     0, c, h * s.dr : (h + 1) * s.dr, l * LANES : (l + 1) * LANES]
         else:
-            ag_a(zr - 1)
-        inner = unpack(x3())
-        wide = jnp.concatenate([inner] * s.lb, axis=1)
-        for h in range(2):
-            ixs[it, h] = jnp.where(hot(h), wide, 0.0).astype(bf16)
-        ix_i = slot()
-        ixc[it, c] = ixs[it, c]
-        push(ixs.at[it, 1 - c], ixc.at[it, c], ix_i, ix_i, partner)
-        if it == 0:
-            for k in range(zh):
-                @pl.when(c * zh + k != z)
-                def _():
-                    landed(base_of(k), a0_r + k)
-        else:
-            ag_a(zr)
-            dn_i = slot()
-            push(a.at[it, :, pl.ds(s.na_base, s.dr)], dnr.at[it], dn_i, dn_i, partner)
-        bt = jnp.concatenate(
-            [a[it, k, i * s.hc : (i + 1) * s.hc, :] for k in range(zh) for i in range(s.nt)], axis=1)
-        if pad_rows:
-            bt = jnp.concatenate([bt, jnp.zeros((pad_rows, s.dh), bf16)], axis=0)
-        xb_i = slot()
-        xb_s[it] = dot_t(calh[oth_rows, :], bt)
-        push(xb_s.at[it], xb_r.at[it], xb_i, xb_i, partner)
-        part = dot_t(calh[own_rows, :], bt)
-        if it > 0:
             landed(dnr.at[it], dn_i)
             for p in range(zh):
                 l, h = p // 2, p % 2
@@ -487,9 +481,9 @@
         ya3()
         last = it == ITERS - 1
         if not last:
-            ag_a = ag_maker(a, it + 1, 0, s.na)
-            for i in range(max(zr - 2, 1)):
-                ag_a(i)
+            ag1, ag2, ag3 = ag_maker(a, it + 1, s.na)
+            pl.when(mine)(ag1)
+            ag2()
         else:
             bf_i, dn_s, dn_r = slot(), slot(Z), slot(zh)
             dn_of = lambda k: a.at[ITERS, k, pl.ds(s.na_base, s.dr)]

time: 159 us -> 148 us (0.931)
  Pallas kernels: 151 us -> 141 us
    pallas_call x1, Pallas kernels: 151 us -> 141 us  [body(): pl.pallas_call(functools.partial(kernel, s, n_sem), out_shape=(jax.ShapeD...]
where the time goes in v4:
time: 148 us; the launch traced here: 147 us
  Pallas kernels  141 us (95%)
  local copies, waits for them, and re-layouts  6.08 us (4%)
    pallas_call x1, Pallas kernels, body(): pl.pallas_call(functools.partial(kernel, s, n_sem), out_shape=(jax.ShapeD...  141 us
    unnamed x3, local copies, waits for them, and re-layouts  4.84 us

profile of v4, /device:TPU:1, one launch (start us, length us, event | category | flops | bytes accessed | tf_op | source)
XLA Modules:
  0.0 147.5 jit_solution(2753748358635317604)
XLA Ops:
  0.6 1.2 broadcast_in_dim.9.route
  1.9 140.8 %refine.1 = (bf16[80,96]{1,0:T(8,128)(2,1)}, bf16[64,5120]{1,0:T(8,128)(2,1)}, bf16[64,768]{1,0:T(8,128)(2,1)}) custom-call(bf16[320,5120]{1,0:T(8,128)(2,1)} %calib.1, bf16[96,320]{1,0:T(8,128)(2,1)} %bitcast.13, s32[1,320]{1,0:T(1,128)} %broadcast_in_dim.9.route, bf16[80,96]{1,0:T(8,128)(2,1)} %base.1, bf16[64,5120]{1,0:T(8,128)(2,1)} %bitcast.9, ...), custom_call_target="tpu_custom_call" | custom-call | tf_op jit(solution)/shard_map/refine/pallas_call | solution.py:583
  142.6 1.3 copy.12
  144.0 2.0 %copy.13 = bf16[1,5120,64]{1,2,0:T(8,128)(2,1)} copy(bf16[1,5120,64]{1,2,0:T(8,128)(2,1)} %bitcast.10) | data formatting | bytes 1310720
  146.0 1.5 %copy.14 = bf16[1,64,768]{2,1,0:T(8,128)(2,1)} copy(bf16[1,64,768]{2,1,0:T(8,128)(2,1)} %bitcast.11) | data formatting | bytes 196608

commit v5 on v4

--- a/solution.py
+++ b/solution.py
@@ -72,8 +72,13 @@
         bo=vm((s.zh, RANK, s.cw), bf16),
         dn=vm((ITERS, 2, s.hc, s.el), bf16),
         dnr=vm((ITERS, s.zh, s.dr, LANES), bf16),
-        ga=vm((ITERS, s.zh, s.na_pad, LANES), bf16),
-        gar=vm((ITERS, Z * YL, s.pa, LANES), bf16),
+        ga=vm((ITERS, s.zh, s.na, LANES), bf16),
+        rly=vm((ITERS, 2, Z // 4, s.na, LANES), bf16),
+        rsum=vm((ITERS, 2, s.na, LANES), bf16),
+        gin=vm((ITERS, 2, Z // 4, s.na, LANES), bf16),
+        ya=vm((YL, s.pa, LANES), f32),
+        yas=vm((ITERS, YL, s.pa, LANES), bf16),
+        yar=vm((ITERS, YL, s.pa, LANES), bf16),
         gb=vm((ITERS, s.zh, RANK, s.cw), bf16),
         gbr=vm((ITERS, Z * YL, s.pb, s.cw), bf16),
         xin_s=vm((ITERS, s.t // 2, LANES), f32),
@@ -98,7 +103,7 @@
 
 def kernel(s, n_sem, calib, target, route, base, up, down, o_base, o_up, o_down, *, send, recv,
            calh, calo, uph, tgt, rou, bas, dwn, bpad, bg, tpad, tcol, rcol, d0s, d0r, a, b, bo, dn, dnr,
-           ga, gar, gb, gbr, xin_s, xin_r, xb_s, xb_r,
+           ga, rly, rsum, gin, ya, yas, yar, gb, gbr, xin_s, xin_r, xb_s, xb_r,
            e1s, e1r, e2s, e2r, ixs, ixc, res, back, bfin, fin, dnf, fdn, local_sem):
     t, zh = s.t, s.zh
     width = 2 * s.dh
@@ -256,8 +261,8 @@
     others = [(dz, dy) for dz in far for dy in range(YL) if dz or dy]
     half_pieces = zh * YL
 
-    def sum_maker(it, buf, g, got, size, everywhere):
-        s1, r1, s2, r2 = slot(), slot(), slot(YL), slot(YL)
+    def sum_maker(it, buf, g, got, size):
+        s1, r1, s2, r2 = slot(), slot(), slot(), slot()
         rows = lambda y_: pl.ds(pl.multiple_of(y_ * size, 16), size)
 
         def some(cnt):
@@ -286,37 +291,115 @@
                 old = buf[it, zi, rows(y), :].astype(f32)
                 buf[it + 1, zi, rows(y), :] = (old - STEP_RATE * val).astype(bf16)
                 piece = buf.at[it + 1, zi, rows(y)]
-                if everywhere:
-                    for dz, dy in others:
-                        rcopy(piece, piece, s2, r2,
-                              (e, row_of((z + dz) % Z, (y + dy) % YL, c))).start()
-                else:
-                    for dy in range(1, YL):
-                        rcopy(piece, piece, s2 + dy, r2 + dy,
-                              (e, row_of(z, (y + dy) % YL, c))).start()
-
-            if everywhere:
-                sends.append((mine, some(Z * YL - 1), s2))
-            else:
+                for dz, dy in others:
+                    rcopy(piece, piece, s2, r2,
+                          (e, row_of((z + dz) % Z, (y + dy) % YL, c))).start()
+
+            sends.append((mine, some(Z * YL - 1), s2))
+
+        def third():
+            @pl.when(mine)
+            def _():
+                landed(got.at[it, pl.ds(1, half_pieces - 1)], r2)
+
+            @pl.when(other_core)
+            def _():
+                landed(got.at[it, pl.ds(1, half_pieces)], r2)
+
+        return first, second, third
+
+    def chunk_sum_maker(it):
+        near = Z // 4
+        n, cut, piece = s.na, s.na // 32 * 16, s.pa
+        s_far, r_far, s_near, r_near = slot(2 * near), slot(2 * near), slot(2 * near), slot(2 * near)
+        s1, r1, s2, r2 = slot(YL), slot(YL), slot(YL), slot(YL)
+        dev = lambda dz: (e, row_of((z + Z + dz) % Z, y, c))
+        rows = lambda y_: pl.ds(pl.multiple_of(y_ * piece, 16), piece)
+
+        def part(i, q):
+            return (0, n) if q < near else ((0, cut) if i == 0 else (cut, n - cut))
+
+        def step1():
+            for q in range(near, 0, -1):
+                for i, sign in enumerate((1, -1)):
+                    d = (z + Z + sign * (q + near)) % Z
+                    on = d // zh == c
+                    lo, m = part(i, q)
+
+                    @pl.when(on)
+                    def _():
+                        push(ga.at[it, d % zh, pl.ds(lo, m)], rly.at[it, i, q - 1, pl.ds(lo, m)],
+                             s_far + 2 * (q - 1) + i, r_far + 2 * (q - 1) + i, dev(sign * q), on,
+                             lambda lo=lo, m=m: ga.at[it, 0, pl.ds(lo, m)])
+
+            for q in range(near - 1, 0, -1):
+                for i, sign in enumerate((1, -1)):
+                    d = (z + Z + sign * q) % Z
+                    on = d // zh == c
+
+                    @pl.when(on)
+                    def _():
+                        push(ga.at[it, d % zh], gin.at[it, i, q - 1], s_near + 2 * (q - 1) + i,
+                             r_near + 2 * (q - 1) + i, dev(sign * q), on, lambda: ga.at[it, 0])
+
+        def step2():
+            for i, sign in enumerate((1, -1)):
+                d = (z + Z + sign * near) % Z
+                on = d // zh == c
+
+                @pl.when(on)
+                def _():
+                    for q in range(near, 0, -1):
+                        lo, m = part(i, q)
+                        landed(rly.at[it, i, q - 1, pl.ds(lo, m)], r_far + 2 * (q - 1) + i)
+                    for lo, m in (part(0, near), part(1, near)):
+                        val = ga[it, d % zh, lo : lo + m, :].astype(f32)
+                        for q in range(1, near + 1):
+                            if q < near or (lo, m) == part(i, near):
+                                val = val + rly[it, i, q - 1, lo : lo + m, :].astype(f32)
+                        rsum[it, i, lo : lo + m, :] = val.astype(bf16)
+                    push(rsum.at[it, i], gin.at[it, i, near - 1], s_near + 2 * (near - 1) + i,
+                         r_near + 2 * (near - 1) + i, dev(sign * near), on, lambda: rsum.at[it, 0])
+
+        def first():
+            @pl.when(mine)
+            def _():
+                val = ga[it, zi].astype(f32)
+                for q in range(1, near + 1):
+                    for i in range(2):
+                        landed(gin.at[it, i, q - 1], r_near + 2 * (q - 1) + i)
+                        val = val + gin[it, i, q - 1].astype(f32)
+                val = jnp.concatenate([val, jnp.zeros((s.na_pad - n, LANES), f32)], axis=0)
+                val = val.reshape(YL, piece, LANES)
+                ya[...] = val
+                yas[it] = val.astype(bf16)
                 for dy in range(1, YL):
-                    sends.append((mine, lambda: got.at[it, 0], s2 + dy))
+                    o = (y + dy) % YL
+                    push(yas.at[it, o], yar.at[it, y], s1 + dy, r1 + dy, (e, row_of(z, o, c)), mine,
+                         lambda: yas.at[it, 0])
+
+        def second():
+            @pl.when(mine)
+            def _():
+                val = ya[y]
+                for dy in range(1, YL):
+                    o = (y + YL - dy) % YL
+                    landed(yar.at[it, o], r1 + dy)
+                    val = val + yar[it, o].astype(f32)
+                old = a[it, zi, rows(y), :].astype(f32)
+                a[it + 1, zi, rows(y), :] = (old - STEP_RATE * val).astype(bf16)
+                new = a.at[it + 1, zi, rows(y)]
+                for dy in range(1, YL):
+                    push(new, new, s2 + dy, r2 + dy, (e, row_of(z, (y + dy) % YL, c)), mine,
+                         lambda: yas.at[it, 0])
 
         def third():
-            if everywhere:
-                @pl.when(mine)
-                def _():
-                    landed(got.at[it, pl.ds(1, half_pieces - 1)], r2)
-
-                @pl.when(other_core)
-                def _():
-                    landed(got.at[it, pl.ds(1, half_pieces)], r2)
-            else:
-                @pl.when(mine)
-                def _():
-                    for dy in range(1, YL):
-                        landed(buf.at[it + 1, zi, rows((y + YL - dy) % YL)], r2 + dy)
-
-        return first, second, third
+            @pl.when(mine)
+            def _():
+                for dy in range(1, YL):
+                    landed(a.at[it + 1, zi, rows((y + YL - dy) % YL)], r2 + dy)
+
+        return step1, step2, first, second, third
 
     def exp_maker(it, w):
         i1, s2, r2 = slot(), slot(X), slot(X)
@@ -461,10 +544,10 @@
             l, h = p // 2, p % 2
             ga[it, p, s.na_base : s.na, :] = grad[
                 h * s.dr : (h + 1) * s.dr, l * LANES : (l + 1) * LANES].astype(bf16)
-        ga[it, :, s.na :, :] = jnp.zeros((zh, s.na_pad - s.na, LANES), bf16)
-        ya1, ya2, ya3 = sum_maker(it, a, ga, gar, s.pa, False)
-        ya1()
+        rs1, rs2, ya1, ya2, ya3 = chunk_sum_maker(it)
+        rs1()
         b2()
+        rs2()
         bk = unpack(b3()).astype(bf16).astype(f32)
         back[it, c] = jnp.where(mask_own, bk, 0.0).astype(bf16)
         bk_i = slot()
@@ -474,8 +557,9 @@
         grad = dot(bt, calh[...]) * inv_t
         for k in range(zh):
             gb[it, k] = grad[:, k * s.cw : (k + 1) * s.cw].astype(bf16)
-        yb1, yb2, yb3 = sum_maker(it, b, gb, gbr, s.pb, True)
+        yb1, yb2, yb3 = sum_maker(it, b, gb, gbr, s.pb)
         yb1()
+        ya1()
         ya2()
         yb2()
         ya3()

time: 148 us -> 143 us (0.966)
  Pallas kernels: 141 us -> 136 us
    pallas_call x1, Pallas kernels: 141 us -> 136 us  [body(): pl.pallas_call(functools.partial(kernel, s, n_sem), out_shape=(jax.ShapeD...]
where the time goes in v5:
time: 143 us; the launch traced here: 142 us
  Pallas kernels  136 us (95%)
  local copies, waits for them, and re-layouts  6.08 us (4%)
    pallas_call x1, Pallas kernels, body(): pl.pallas_call(functools.partial(kernel, s, n_sem), out_shape=(jax.ShapeD...  136 us
    unnamed x3, local copies, waits for them, and re-layouts  4.84 us

profile of v5, /device:TPU:1, one launch (start us, length us, event | category | flops | bytes accessed | tf_op | source)
XLA Modules:
  0.0 142.3 jit_solution(16047491370004188488)
XLA Ops:
  0.6 1.2 broadcast_in_dim.9.route
  1.9 135.6 %refine.1 = (bf16[80,96]{1,0:T(8,128)(2,1)}, bf16[64,5120]{1,0:T(8,128)(2,1)}, bf16[64,768]{1,0:T(8,128)(2,1)}) custom-call(bf16[320,5120]{1,0:T(8,128)(2,1)} %calib.1, bf16[96,320]{1,0:T(8,128)(2,1)} %bitcast.13, s32[1,320]{1,0:T(1,128)} %broadcast_in_dim.9.route, bf16[80,96]{1,0:T(8,128)(2,1)} %base.1, bf16[64,5120]{1,0:T(8,128)(2,1)} %bitcast.9, ...), custom_call_target="tpu_custom_call" | custom-call | tf_op jit(solution)/shard_map/refine/pallas_call | solution.py:667
  137.5 1.3 copy.12
  138.8 2.0 %copy.13 = bf16[1,5120,64]{1,2,0:T(8,128)(2,1)} copy(bf16[1,5120,64]{1,2,0:T(8,128)(2,1)} %bitcast.10) | data formatting | bytes 1310720
  140.8 1.5 %copy.14 = bf16[1,64,768]{2,1,0:T(8,128)(2,1)} copy(bf16[1,64,768]{2,1,0:T(8,128)(2,1)} %bitcast.11) | data formatting | bytes 196608

commit v6 on v5

--- a/solution.py
+++ b/solution.py
@@ -615,6 +615,10 @@
     rows = pl.ds(pl.multiple_of((2 * y + c) * s.db, 16), s.db)
     o_base[...] = fin[rows, :][:, : s.hc].astype(bf16)
 
+    yb3()
+    fb = slot()
+    push(b.at[ITERS], bo, fb, fb, partner)
+
     owner = x // s.lb == c
 
     @pl.when(owner)
@@ -624,10 +628,6 @@
             def _():
                 landed(dnf.at[j], fr + j)
         push(dnf, dnf, fc, fc, partner, owner)
-
-    yb3()
-    fb = slot()
-    push(b.at[ITERS], bo, fb, fb, partner)
 
     @pl.when(jnp.logical_not(owner))
     def _():

time: 143 us -> 142 us (level)
  no operation moved by 1% of the time
where the time goes in v6:
time: 142 us
  Pallas kernels  135 us (95%)
  local copies, waits for them, and re-layouts  6.08 us (4%)
    pallas_call x1, Pallas kernels, body(): pl.pallas_call(functools.partial(kernel, s, n_sem), out_shape=(jax.ShapeD...  135 us
    unnamed x3, local copies, waits for them, and re-layouts  4.84 us

profile of v6, /device:TPU:1, one launch (start us, length us, event | category | flops | bytes accessed | tf_op | source)
XLA Modules:
  0.0 142.1 jit_solution(13116871342504399764)
XLA Ops:
  0.6 1.2 broadcast_in_dim.9.route
  1.9 135.4 %refine.1 = (bf16[80,96]{1,0:T(8,128)(2,1)}, bf16[64,5120]{1,0:T(8,128)(2,1)}, bf16[64,768]{1,0:T(8,128)(2,1)}) custom-call(bf16[320,5120]{1,0:T(8,128)(2,1)} %calib.1, bf16[96,320]{1,0:T(8,128)(2,1)} %bitcast.13, s32[1,320]{1,0:T(1,128)} %broadcast_in_dim.9.route, bf16[80,96]{1,0:T(8,128)(2,1)} %base.1, bf16[64,5120]{1,0:T(8,128)(2,1)} %bitcast.9, ...), custom_call_target="tpu_custom_call" | custom-call | tf_op jit(solution)/shard_map/refine/pallas_call | solution.py:667
  137.2 1.3 copy.12
  138.6 2.0 %copy.13 = bf16[1,5120,64]{1,2,0:T(8,128)(2,1)} copy(bf16[1,5120,64]{1,2,0:T(8,128)(2,1)} %bitcast.10) | data formatting | bytes 1310720
  140.5 1.5 %copy.14 = bf16[1,64,768]{2,1,0:T(8,128)(2,1)} copy(bf16[1,64,768]{2,1,0:T(8,128)(2,1)} %bitcast.11) | data formatting | bytes 196608
